TPU v7x, 256 devices: a whole 4x4x8 slice. The times are simulated.
256 devices in a mesh: dp: 2 (over y_hi), expert: 128 (over x, y_lo, z, core).
Axes of the slice: x: 4, y: 4 (y_hi: 2, y_lo: 2; y = y_hi * 2 + y_lo), z: 8, core: 2. Of those that a mesh axis runs over, the one named last changes fastest.
Arguments:
- tokens: bfloat16 [512, 256, 1280], P(('dp', 'expert')), may hold values from -6 to 6
- norm_gain: float32 [1280], replicated, may hold values from 0.1 to 1.9
- slot_params: bfloat16 [1280, 128], replicated, may hold values from -0.15625 to 0.15625
- logit_scale: float32 [1], replicated, may hold values from 24 to 72
- expert_up: bfloat16 [128, 2560, 1280], P('expert', 'dp'), may hold values from -1.25 to 1.25
- expert_down: bfloat16 [128, 2560, 1280], P('expert', 'dp'), may hold values from -0.3125 to 0.3125
Outputs:
- mixed: bfloat16 [512, 256, 1280], P(('dp', 'expert'))
All inputs are finite; a program needn't handle non-finite values.
Results may differ from a plain program's by a relative error of at most 0.019.
Values may be sent and summed in bfloat16 or wider, within the bound.
No kernel may reach another device: no remote copies, remote signals or barrier semaphores. Data moves between devices by JAX's collectives and lax.ppermute only.
A program may use at most 64 MiB of HBM per device.

v0:
```python
import jax
import jax.numpy as jnp
from jax import lax
from jax.sharding import PartitionSpec as P


def normalize_tokens(values, norm_gain):
    floats = values.astype(jnp.float32)
    centred = floats - jnp.mean(floats, axis=-1, keepdims=True)
    variance = jnp.mean(centred * centred, axis=-1, keepdims=True)
    return (centred * lax.rsqrt(variance + 1e-06) * norm_gain).astype(jnp.bfloat16)


def local(tokens, norm_gain, slot_params, logit_scale, expert_up, expert_down):
    width = tokens.shape[-1]
    normed = normalize_tokens(tokens, norm_gain)
    scores = jnp.einsum("itd,ds->its", normed, slot_params, preferred_element_type=jnp.float32)
    normed_f = normed.astype(jnp.float32)
    params_f = slot_params.astype(jnp.float32)
    token_norm = jnp.sqrt(jnp.sum(normed_f * normed_f, axis=-1) + 1e-06)
    param_norm = jnp.sqrt(jnp.sum(params_f * params_f, axis=0) + 1e-06)
    logits = logit_scale[0] * scores / (token_norm[:, :, None] * param_norm[None, None, :])
    expo = jnp.exp(logits)
    dispatch = (expo / jnp.sum(expo, axis=1, keepdims=True)).astype(jnp.bfloat16)
    combine = (expo / jnp.sum(expo, axis=2, keepdims=True)).astype(jnp.bfloat16)
    slot_inputs = jnp.einsum(
        "its,itd->sid", dispatch, normed, preferred_element_type=jnp.float32
    ).astype(jnp.bfloat16)
    up_matrix = expert_up[0]
    down_matrix = expert_down[0]
    arrived = lax.all_to_all(slot_inputs, "expert", split_axis=0, concat_axis=0, tiled=True)
    gathered = lax.all_gather(arrived, "dp", axis=0, tiled=True)
    slot_rows = gathered.reshape(-1, width)
    hidden = jax.nn.gelu(
        lax.dot_general(
            slot_rows, up_matrix, (((1,), (1,)), ((), ())), preferred_element_type=jnp.float32
        ),
        approximate=False,
    ).astype(jnp.bfloat16)
    partial_out = (
        jnp.dot(hidden, down_matrix, preferred_element_type=jnp.float32)
        .reshape(gathered.shape)
        .astype(jnp.bfloat16)
    )
    returned = lax.all_to_all(
        lax.psum_scatter(partial_out, "dp", scatter_dimension=0, tiled=True)
        .astype(jnp.float32)
        .astype(jnp.bfloat16),
        "expert",
        split_axis=0,
        concat_axis=0,
        tiled=True,
    )
    return jnp.einsum("its,sid->itd", combine, returned, preferred_element_type=jnp.float32).astype(
        jnp.bfloat16
    )


def solution(mesh):
    placed = (
        P(("dp", "expert"), None, None),
        P(),
        P(),
        P(),
        P("expert", "dp", None),
        P("expert", "dp", None),
    )
    return jax.shard_map(
        local,
        mesh=mesh,
        in_specs=placed,
        out_specs=P(("dp", "expert"), None, None),
        check_vma=False,
    )
```

profile of v0, /device:TPU:1, one launch (start us, length us, event | category | flops | bytes accessed | tf_op | source)
XLA Modules:
  0.0 179.8 jit_solution(14880402353378480036)
XLA Ops:
  6.5 0.0 copy-start
  6.5 0.0 copy-start.3
  6.5 0.0 all-gather.2.cloned.1.call-start
  6.5 0.0 copy-start.1
  6.5 0.0 copy-start.2
  7.4 1.3 multiply_reduce_fusion.1
  8.7 1.6 convert_reduce_fusion
  10.2 1.8 fusion.9
  12.1 0.0 copy-done.3
  12.1 0.0 copy-done.1
  12.1 0.7 multiply_reduce_fusion
  12.8 0.0 copy-done.2
  12.8 0.6 fusion.27
  13.4 3.1 %fusion.24 = bf16[128,2,1280]{0,2,1:T(8,128)(2,1)} fusion(bf16[2,256,1280]{2,1,0:T(8,128)(2,1)} %param.6, f32[1280]{0:T(1024)S(1)} %copy-done.3, f32[2,256]{1,0:T(2,128)S(1)} %add_rsqrt_fusion, f32[2,256]{1,0:T(2,128)S(1)} %broadcast_multiply_fusion, f32[2,256,128]{2,1,0:T(8,128)S(1)} %fusion.27), kind=kOutput, calls=%fused_computation.34 | convolution fusion | flops 171508224 | bytes 2237440 | tf_op jit(solution)/shard_map/its,itd->sid/dot_general | solution.py:26
  16.4 3.0 %copy.16 = bf16[128,2,1280]{2,1,0:T(2,128)(2,1)} copy(bf16[128,2,1280]{0,2,1:T(8,128)(2,1)} %fusion.24) | data formatting | bytes 1310720 | tf_op jit(solution)/shard_map/convert_element_type | solution.py:28
  19.4 37.6 %all_to_all.10 = bf16[128,2,1280]{2,1,0:T(2,128)(2,1)} all-to-all(bf16[128,2,1280]{2,1,0:T(2,128)(2,1)} %copy.16), channel_id=1, replica_groups=mesh['dp'=2,'expert'=128] {'expert'}, dimensions={0} | all-to-all | bytes 1310720 | tf_op jit(solution)/shard_map/all_to_all | solution.py:31
  57.0 0.0 all-gather.2.cloned.1.call-update
  57.0 0.2 reduce-scatter.2.cloned.1.call-start
  57.3 25.5 %all-gather.2.cloned.1.call-done = bf16[256,2,1280]{2,1,0:T(2,128)(2,1)} async-done(((bf16[128,2,1280]{2,1,0:T(2,128)(2,1)}), bf16[256,2,1280]{2,1,0:T(2,128)(2,1)}) %all-gather.2.cloned.1.call-update) | async-done | bytes 1310736 | tf_op jit(solution)/shard_map/all_gather | solution.py:32
  82.8 4.1 %reshape.28 = bf16[512,1280]{1,0:T(8,128)(2,1)} reshape(bf16[256,2,1280]{2,1,0:T(2,128)(2,1)} %all-gather.2.cloned.1.call-done) | data formatting | bytes 2621440 | tf_op jit(solution)/shard_map/reshape | solution.py:33
  86.8 0.0 copy-done
  86.8 9.0 %fusion.14 = bf16[512,1280]{1,0:T(8,128)(2,1)} fusion(bf16[512,1280]{1,0:T(8,128)(2,1)} %reshape.28, bf16[1,1280,1280]{2,1,0:T(8,128)(2,1)S(1)} %copy-done), kind=kOutput, calls=%fused_computation.16 | convolution fusion | flops 1720320000 | bytes 5898240 | tf_op jit(solution)/shard_map/dot_general | solution.py:35
  95.8 4.0 %dot_general.20 = bf16[256,2,1280]{2,1,0:T(2,128)(2,1)} reshape(bf16[512,1280]{1,0:T(8,128)(2,1)} %fusion.14) | data formatting | bytes 2621440 | tf_op jit(solution)/shard_map/dot_general | solution.py:41
  99.8 5.2 %fusion.6 = bf16[256,2,1280]{2,0,1:T(8,128)(2,1)} fusion(bf16[1,1280,1280]{2,1,0:T(8,128)(2,1)} %param.11, bf16[256,2,1280]{2,1,0:T(2,128)(2,1)} %dot_general.20), kind=kOutput, calls=%fused_computation.9 | convolution fusion | flops 1678376960 | bytes 5898240 | tf_op jit(solution)/shard_map/dot_general | solution.py:41
  105.0 0.0 reduce-scatter.2.cloned.1.call-update
  105.1 29.4 %reduce-scatter.2.cloned.1.call-done = bf16[128,2,1280]{2,0,1:T(8,128)(2,1)} async-done(((bf16[256,2,1280]{2,0,1:T(8,128)(2,1)}), bf16[128,2,1280]{2,0,1:T(8,128)(2,1)}) %reduce-scatter.2.cloned.1.call-update) | async-done | bytes 655376 | tf_op jit(solution)/shard_map/reduce_scatter | solution.py:46
  134.5 1.8 copy.18
  136.2 34.1 %all_to_all.11 = bf16[128,2,1280]{2,1,0:T(2,128)(2,1)} all-to-all(bf16[128,2,1280]{2,1,0:T(2,128)(2,1)S(1)} %copy.18), channel_id=1, replica_groups=mesh['dp'=2,'expert'=128] {'expert'}, dimensions={0} | all-to-all | bytes 1310720 | tf_op jit(solution)/shard_map/all_to_all | solution.py:45
  170.3 2.7 %convolution_convert_fusion = bf16[2,256,1280]{2,1,0:T(8,128)(2,1)} fusion(bf16[128,2,1280]{2,1,0:T(2,128)(2,1)} %all_to_all.11, f32[2,256,128]{2,1,0:T(8,128)S(1)} %fusion.27), kind=kOutput, calls=%fused_computation.10 | convolution fusion | flops 168559232 | bytes 2228224 | tf_op jit(solution)/shard_map/its,sid->itd/dot_general | solution.py:54
  (4 shorter events, 0.0 us)
Async XLA Ops:
  6.5 80.3 %copy-start = (bf16[1,1280,1280]{2,1,0:T(8,128)(2,1)S(1)}, bf16[1,1280,1280]{2,1,0:T(8,128)(2,1)}, u32[]{:S(2)}) copy-start(bf16[1,1280,1280]{2,1,0:T(8,128)(2,1)} %param.10) | copy-start | bytes 9830404
  6.5 5.5 %copy-start.3 = (f32[1280]{0:T(1024)S(1)}, f32[1280]{0:T(1024)}, u32[]{:S(2)}) copy-start(f32[1280]{0:T(1024)} %param.7) | copy-start | bytes 15364
  6.5 76.2 %all-gather.2.cloned.1.call-start = ((), (), s32[]{:S(2)}) async-start(), calls=%async_computation.3 | async-start | bytes 1966080 | tf_op jit(solution)/shard_map/all_gather | solution.py:32
  6.5 5.5 %copy-start.1 = (bf16[2,256,1280]{2,1,0:T(8,128)(2,1)S(1)}, bf16[2,256,1280]{2,1,0:T(8,128)(2,1)}, u32[]{:S(2)}) copy-start(bf16[2,256,1280]{2,1,0:T(8,128)(2,1)} %param.6) | copy-start | bytes 3932164
  6.5 6.2 %copy-start.2 = (bf16[1280,128]{1,0:T(8,128)(2,1)S(1)}, bf16[1280,128]{1,0:T(8,128)(2,1)}, u32[]{:S(2)}) copy-start(bf16[1280,128]{1,0:T(8,128)(2,1)} %param.8) | copy-start | bytes 983044
  57.0 77.4 %reduce-scatter.2.cloned.1.call-start = ((), (), s32[]{:S(2)}) async-start(), calls=%async_computation.4 | async-start | bytes 1966080 | tf_op jit(solution)/shard_map/reduce_scatter | solution.py:46
Sparse Core Ops, SparseCore 0:
  57.2 25.5 all-gather.1
  105.2 29.2 reduce-scatter.1
where the time goes:
time: 180 us
  blocking collectives  71.6 us (40%)
  waiting for transfers between devices  54.9 us (30%)
  matrix products  20.6 us (11%)
  between operations  14.3 us (8%)
  local copies, waits for them, and re-layouts  12.8 us (7%)
  other arithmetic  5.37 us (3%)
    all_to_all x1, blocking collectives, local(): lax.all_to_all(slot_inputs, 'expert', split_axis=0, concat_axis=0, tiled=...  37.6 us
    all_to_all x1, blocking collectives, local(): lax.all_to_all(lax.psum_scatter(partial_out, 'dp', scatter_dimension=0, t...  34.1 us
    reduce_scatter x1, waiting for transfers between devices, local(): lax.psum_scatter(partial_out, 'dp', scatter_dimension=0, tiled=True)  29.4 us
    all_gather x1, waiting for transfers between devices, local(): gathered = lax.all_gather(arrived, 'dp', axis=0, tiled=True)  25.5 us
    dot_general x1, matrix products, local(): lax.dot_general(slot_rows, up_matrix, (((1,), (1,)), ((), ())), preferred...  9 us
    dot_general x1, matrix products, local(): jnp.dot(hidden, down_matrix, preferred_element_type=jnp.float32)  5.25 us
    reshape x1, local copies, waits for them, and re-layouts, local(): slot_rows = gathered.reshape(-1, width)  4.06 us
    dot_general x1, local copies, waits for them, and re-layouts, local(): jnp.dot(hidden, down_matrix, preferred_element_type=jnp.float32)  3.95 us
  transfers between devices with their start and end apart: 2, of which 2 were waited for; matrix products, arithmetic and copies ran while one was open for 0% of the time, Pallas kernels for 0%

commit v1 on v0

v1 whole, which is shorter than its diff:
```python
import jax
import jax.numpy as jnp
from jax import lax
from jax.experimental import pallas as pl
from jax.experimental.pallas import tpu as pltpu
from jax.sharding import PartitionSpec as P

BF16 = jnp.bfloat16
F32 = jnp.float32
VMEM_LIMIT = 24 * 1024 * 1024


def halves(value):
    middle = value.shape[-1] // 2
    return value[:, :middle], value[:, middle:]


def route_kernel(tokens_ref, gain_ref, params_ref, scale_ref, slots_ref, combine_ref, normed_ref):
    tokens, width = normed_ref.shape
    gain = gain_ref[...]
    norms = []
    block = 64
    for at in range(0, tokens, block):
        rows = pl.ds(at, block)
        floats = tokens_ref[0, rows, :].astype(F32)
        centred = floats - jnp.mean(floats, axis=-1, keepdims=True)
        variance = jnp.mean(centred * centred, axis=-1, keepdims=True)
        normed = (centred * lax.rsqrt(variance + 1e-06) * gain).astype(BF16)
        normed_ref[rows, :] = normed
        normed_f = normed.astype(F32)
        norms.append(jnp.sum(normed_f * normed_f, axis=-1, keepdims=True))
    token_norm = jnp.sqrt(jnp.concatenate(norms, axis=0) + 1e-06)
    params = params_ref[...]
    params_f = params.astype(F32)
    param_norm = jnp.sqrt(jnp.sum(params_f * params_f, axis=0, keepdims=True) + 1e-06)
    normed = normed_ref[...]
    scores = jnp.dot(normed, params, preferred_element_type=F32)
    logits = scale_ref[0] * scores / (token_norm * param_norm)
    expo = jnp.exp(logits)
    dispatch = (expo / jnp.sum(expo, axis=0, keepdims=True)).astype(BF16)
    combine_ref[...] = (expo / jnp.sum(expo, axis=1, keepdims=True)).astype(BF16)
    slots = lax.dot_general(
        dispatch, normed, (((0,), (0,)), ((), ())), preferred_element_type=F32
    ).astype(BF16)
    slots_ref[:, 0, :], slots_ref[:, 1, :] = halves(slots)


def route(tokens, norm_gain, slot_params, logit_scale, image):
    _, count, width = tokens.shape
    slots = slot_params.shape[1]
    return pl.pallas_call(
        route_kernel,
        grid=(1,),
        in_specs=[
            pl.BlockSpec((1, count, width), lambda i: (image, 0, 0)),
            pl.BlockSpec((1, width), lambda i: (0, 0)),
            pl.BlockSpec((width, slots), lambda i: (0, 0)),
            pl.BlockSpec(memory_space=pltpu.SMEM),
        ],
        out_specs=[
            pl.BlockSpec((slots, 2, width // 2), lambda i: (0, 0, 0)),
            pl.BlockSpec((count, slots), lambda i: (0, 0)),
        ],
        out_shape=[
            jax.ShapeDtypeStruct((slots, 2, width // 2), BF16),
            jax.ShapeDtypeStruct((count, slots), BF16),
        ],
        scratch_shapes=[pltpu.VMEM((count, width), BF16)],
        compiler_params=pltpu.CompilerParams(vmem_limit_bytes=VMEM_LIMIT),
        cost_estimate=pl.CostEstimate(
            flops=4 * count * width * slots, bytes_accessed=2 * count * width * 2, transcendentals=count * slots
        ),
        name="route",
    )(tokens, norm_gain.reshape(1, width), slot_params, logit_scale)


def expert_kernel(rows_ref, up_ref, down_ref, out_ref):
    left, right = rows_ref[:, 0, :], rows_ref[:, 1, :]
    middle = left.shape[-1]
    hidden_units = up_ref.shape[1]
    block = 256
    total = None
    for at in range(0, hidden_units, block):
        units = pl.ds(at, block)
        over_features = (((1,), (1,)), ((), ()))
        before = lax.dot_general(
            left, up_ref[0, units, :middle], over_features, preferred_element_type=F32
        ) + lax.dot_general(right, up_ref[0, units, middle:], over_features, preferred_element_type=F32)
        hidden = (before * (0.5 + 0.5 * lax.erf(before * (0.5**0.5)))).astype(BF16)
        term = jnp.dot(hidden, down_ref[0, units, :], preferred_element_type=F32)
        total = term if total is None else total + term
    out_ref[:, 0, :], out_ref[:, 1, :] = halves(total.astype(BF16))


def expert(rows, up_matrix, down_matrix):
    count = rows.shape[0]
    _, hidden_units, width = up_matrix.shape
    vmem = pl.BlockSpec(memory_space=pltpu.VMEM)
    return pl.pallas_call(
        expert_kernel,
        in_specs=[vmem, vmem, vmem],
        out_specs=vmem,
        out_shape=jax.ShapeDtypeStruct(rows.shape, BF16),
        compiler_params=pltpu.CompilerParams(vmem_limit_bytes=VMEM_LIMIT),
        cost_estimate=pl.CostEstimate(
            flops=4 * count * width * hidden_units,
            bytes_accessed=4 * hidden_units * width,
            transcendentals=count * hidden_units,
        ),
        name="expert",
    )(rows, up_matrix, down_matrix)


def mix_kernel(combine_ref, slots_ref, *refs):
    out_ref = refs[-1]
    middle = slots_ref.shape[-1]
    combine = combine_ref[...]
    for half in range(2):
        out_ref[0, :, half * middle : (half + 1) * middle] = jnp.dot(
            combine, slots_ref[:, half, :], preferred_element_type=F32
        ).astype(BF16)


def mix(combine, slot_outputs, image, images, earlier):
    count, slots = combine.shape
    width = 2 * slot_outputs.shape[-1]
    operands = [combine, slot_outputs] + ([] if earlier is None else [earlier])
    in_specs = [
        pl.BlockSpec((count, slots), lambda i: (0, 0)),
        pl.BlockSpec(slot_outputs.shape, lambda i: (0, 0, 0)),
    ] + ([] if earlier is None else [pl.BlockSpec(memory_space=pl.ANY)])
    return pl.pallas_call(
        mix_kernel,
        grid=(1,),
        in_specs=in_specs,
        out_specs=pl.BlockSpec((1, count, width), lambda i: (image, 0, 0)),
        out_shape=jax.ShapeDtypeStruct((images, count, width), BF16),
        input_output_aliases={} if earlier is None else {2: 0},
        compiler_params=pltpu.CompilerParams(vmem_limit_bytes=VMEM_LIMIT),
        cost_estimate=pl.CostEstimate(
            flops=2 * count * width * slots, bytes_accessed=2 * count * width, transcendentals=0
        ),
        name="mix",
    )(*operands)


def swap_dp(value):
    return lax.ppermute(value, "dp", [(0, 1), (1, 0)])


def exchange(value):
    return lax.all_to_all(value, "expert", split_axis=0, concat_axis=0, tiled=True)


def local(tokens, norm_gain, slot_params, logit_scale, expert_up, expert_down):
    images = tokens.shape[0]
    combines, mixed = [], None
    returned = []
    for image in range(images):
        slot_inputs, combine = route(tokens, norm_gain, slot_params, logit_scale, image)
        combines.append(combine)
        arrived = exchange(slot_inputs)
        partner = swap_dp(arrived)
        kept = expert(arrived, expert_up, expert_down)
        received = swap_dp(expert(partner, expert_up, expert_down))
        slot_outputs = (kept.astype(F32) + received.astype(F32)).astype(BF16)
        returned.append(exchange(slot_outputs))
    for image in range(images):
        mixed = mix(combines[image], returned[image], image, images, mixed)
    return mixed


def solution(mesh):
    placed = (
        P(("dp", "expert"), None, None),
        P(),
        P(),
        P(),
        P("expert", "dp", None),
        P("expert", "dp", None),
    )
    return jax.shard_map(
        local,
        mesh=mesh,
        in_specs=placed,
        out_specs=P(("dp", "expert"), None, None),
        check_vma=False,
    )
```

time: 180 us -> 130 us (0.72)
  blocking collectives: 71.6 us -> 30.7 us
  starting transfers between devices: 0.22 us -> 34.8 us
  waiting for transfers between devices: 54.9 us -> 26.6 us
  Pallas kernels: 0 us -> 24.1 us
  matrix products: 20.6 us -> 0 us
  between operations: 14.3 us -> 0.78 us
  local copies, waits for them, and re-layouts: 12.8 us -> 9.48 us
  other arithmetic: 5.37 us -> 3.1 us
    all_to_all x2 -> x1, blocking collectives: 71.6 us -> 30.7 us  [exchange(): lax.all_to_all(value, 'expert', split_axis=0, concat_axis=0, tiled=True)]
    reduce_scatter x1 -> x0, waiting for transfers between devices: 29.4 us -> none  [local(): lax.psum_scatter(partial_out, 'dp', scatter_dimension=0, tiled=True)]
    all_to_all x0 -> x3, starting transfers between devices: none -> 29.3 us  [exchange(): lax.all_to_all(value, 'expert', split_axis=0, concat_axis=0, tiled=True)]
    all_gather x1 -> x0, waiting for transfers between devices: 25.5 us -> none  [local(): gathered = lax.all_gather(arrived, 'dp', axis=0, tiled=True)]
    pallas_call x0 -> x8, Pallas kernels: none -> 24.1 us  [the longest x4 16.9 us: expert(): pl.pallas_call(expert_kernel, in_specs=[vmem, vmem, vmem], out_specs=vmem...]
    dot_general x5 -> x0, matrix products: 20.6 us -> none  [the longest x1 9 us: local(): lax.dot_general(slot_rows, up_matrix, (((1,), (1,)), ((), ())), preferred...]
    all_to_all x0 -> x3, waiting for transfers between devices: none -> 20.2 us  [exchange(): lax.all_to_all(value, 'expert', split_axis=0, concat_axis=0, tiled=True)]
    unnamed x8 -> x14, local copies, waits for them, and re-layouts: 0.02 us -> 8.78 us
  transfers between devices with their start and end apart: 2 -> 7, of which waited for: 2 -> 3; matrix products, arithmetic and copies ran while one was open for 0% -> 2% of each run, Pallas kernels for 0% -> 16%
where the time goes in v1:
time: 130 us; the launch traced here: 129 us
  starting transfers between devices  34.8 us (27%)
  blocking collectives  30.7 us (24%)
  waiting for transfers between devices  26.6 us (20%)
  Pallas kernels  24.1 us (19%)
  local copies, waits for them, and re-layouts  9.48 us (7%)
  other arithmetic  3.1 us (2%)
    all_to_all x1, blocking collectives, exchange(): lax.all_to_all(value, 'expert', split_axis=0, concat_axis=0, tiled=True)  30.7 us
    all_to_all x3, starting transfers between devices, exchange(): lax.all_to_all(value, 'expert', split_axis=0, concat_axis=0, tiled=True)  29.3 us
    all_to_all x3, waiting for transfers between devices, exchange(): lax.all_to_all(value, 'expert', split_axis=0, concat_axis=0, tiled=True)  20.2 us
    pallas_call x4, Pallas kernels, expert(): pl.pallas_call(expert_kernel, in_specs=[vmem, vmem, vmem], out_specs=vmem...  16.9 us
    unnamed x14, local copies, waits for them, and re-layouts  8.78 us
    ppermute x4, waiting for transfers between devices, swap_dp(): return lax.ppermute(value, 'dp', [(0, 1), (1, 0)])  6.4 us
    ppermute x4, starting transfers between devices, swap_dp(): return lax.ppermute(value, 'dp', [(0, 1), (1, 0)])  5.49 us
    pallas_call x2, Pallas kernels, mix(): pl.pallas_call(mix_kernel, grid=(1,), in_specs=in_specs, out_specs=pl.Blo...  4.72 us
  transfers between devices with their start and end apart: 7, of which 3 were waited for; matrix products, arithmetic and copies ran while one was open for 2% of the time, Pallas kernels for 16%

profile of v1, /device:TPU:1, one launch (start us, length us, event | category | flops | bytes accessed | tf_op | source)
XLA Modules:
  0.0 129.5 jit_solution(4719907127010602832)
XLA Ops:
  0.7 0.7 reshape.4.gain_ref
  1.4 1.3 %copy-done.4 = bf16[2,256,1280]{2,1,0:T(8,128)(2,1)S(1)} copy-done((bf16[2,256,1280]{2,1,0:T(8,128)(2,1)S(1)}, bf16[2,256,1280]{2,1,0:T(8,128)(2,1)}, u32[]{:S(2)}) %copy-start.4) | copy-done | bytes 1310744
  2.7 1.0 copy-done.5
  3.6 1.2 route.3
  4.9 30.7 %all_to_all.20.rows_ref = bf16[128,2,640]{2,1,0:T(2,128)(2,1)} all-to-all(bf16[128,2,640]{2,1,0:T(2,128)(2,1)S(1)} %get-tuple-element.12), channel_id=1, replica_groups=mesh['dp'=2,'expert'=128] {'expert'}, dimensions={0} | all-to-all | bytes 655360 | tf_op jit(solution)/shard_map/all_to_all | solution.py:152
  35.5 2.6 %collective-permute-start.2 = (bf16[128,2,640]{2,1,0:T(2,128)(2,1)}, bf16[128,2,640]{2,1,0:T(2,128)(2,1)}, u32[]{:S(2)}, u32[]{:S(2)}) collective-permute-start(bf16[128,2,640]{2,1,0:T(2,128)(2,1)} %all_to_all.20.rows_ref), channel_id=1, source_target_pairs={{0,128},{128,0},{1,129},{129,1},{2,130},{130,2},{3,131},{131,3},{4... | collective-permute-start | bytes 983048 | tf_op jit(solution)/shard_map/ppermute | solution.py:148
  38.2 1.2 route.2
  39.4 0.0 copy-start.6
  39.4 0.7 copy-done.6
  40.1 6.7 %all-to-all-start = ((bf16[128,2,640]{2,1,0:T(2,128)(2,1)}), bf16[128,2,640]{2,1,0:T(2,128)(2,1)}, u32[]{:S(2)}, u32[]{:S(2)}) async-start(bf16[128,2,640]{2,1,0:T(2,128)(2,1)} %copy-done.6), calls=%async_computation | async-start | bytes 655360 | tf_op jit(solution)/shard_map/all_to_all | solution.py:152
  46.9 0.0 collective-permute-done.2.rows_ref
  46.9 0.0 copy-start.1
  46.9 1.9 %copy-done.1 = bf16[1,1280,1280]{2,1,0:T(8,128)(2,1)S(1)} copy-done((bf16[1,1280,1280]{2,1,0:T(8,128)(2,1)S(1)}, bf16[1,1280,1280]{2,1,0:T(8,128)(2,1)}, u32[]{:S(2)}) %copy-start.1) | copy-done | bytes 3276824
  48.8 4.8 %expert.7 = bf16[128,2,640]{2,1,0:T(2,128)(2,1)} custom-call(bf16[128,2,640]{2,1,0:T(2,128)(2,1)} %collective-permute-done.2.rows_ref, bf16[1,1280,1280]{2,1,0:T(8,128)(2,1)S(1)} %copy-done, bf16[1,1280,1280]{2,1,0:T(8,128)(2,1)S(1)} %copy-done.1), custom_call_target="tpu_custom_call" | custom-call | flops 838860800 | bytes 6553600 | tf_op jit(solution)/shard_map/expert/pallas_call | solution.py:99
  53.6 2.1 %collective-permute-start.3 = (bf16[128,2,640]{2,1,0:T(2,128)(2,1)}, bf16[128,2,640]{2,1,0:T(2,128)(2,1)}, u32[]{:S(2)}, u32[]{:S(2)}) collective-permute-start(bf16[128,2,640]{2,1,0:T(2,128)(2,1)} %expert.7), channel_id=1, source_target_pairs={{0,128},{128,0},{1,129},{129,1},{2,130},{130,2},{3,131},{131,3},{4... | collective-permute-start | bytes 983048 | tf_op jit(solution)/shard_map/ppermute | solution.py:148
  55.7 7.1 %all-to-all-done.rows_ref = bf16[128,2,640]{2,1,0:T(2,128)(2,1)} async-done(((bf16[128,2,640]{2,1,0:T(2,128)(2,1)}), bf16[128,2,640]{2,1,0:T(2,128)(2,1)}, u32[]{:S(2)}, u32[]{:S(2)}) %all-to-all-start) | async-done | bytes 327712 | tf_op jit(solution)/shard_map/all_to_all | solution.py:152
  62.8 0.4 collective-permute-start
  63.1 1.9 %copy-done.2 = bf16[1,1280,1280]{2,1,0:T(8,128)(2,1)S(1)} copy-done((bf16[1,1280,1280]{2,1,0:T(8,128)(2,1)S(1)}, bf16[1,1280,1280]{2,1,0:T(8,128)(2,1)}, u32[]{:S(2)}) %copy-start.2) | copy-done | bytes 3276824
  65.0 4.0 %expert.6 = bf16[128,2,640]{2,1,0:T(2,128)(2,1)S(1)} custom-call(bf16[128,2,640]{2,1,0:T(2,128)(2,1)} %all_to_all.20.rows_ref, bf16[1,1280,1280]{2,1,0:T(8,128)(2,1)S(1)} %copy-done, bf16[1,1280,1280]{2,1,0:T(8,128)(2,1)S(1)} %copy-done.2), custom_call_target="tpu_custom_call" | custom-call | flops 838860800 | bytes 6553600 | tf_op jit(solution)/shard_map/expert/pallas_call | solution.py:99
  69.1 2.0 %add_convert_fusion = bf16[128,2,640]{2,1,0:T(2,128)(2,1)} fusion(bf16[128,2,640]{2,1,0:T(2,128)(2,1)} %collective-permute-done.3, bf16[128,2,640]{2,1,0:T(2,128)(2,1)S(1)} %expert.6), kind=kLoop, calls=%fused_computation | loop fusion | flops 655360 | bytes 983040 | tf_op jit(solution)/shard_map/convert_element_type | solution.py:166
  71.1 9.7 %all-to-all-start.3 = ((bf16[128,2,640]{2,1,0:T(2,128)(2,1)}), bf16[128,2,640]{2,1,0:T(2,128)(2,1)}, u32[]{:S(2)}, u32[]{:S(2)}) async-start(bf16[128,2,640]{2,1,0:T(2,128)(2,1)} %add_convert_fusion), calls=%async_computation.3 | async-start | bytes 655360 | tf_op jit(solution)/shard_map/all_to_all | solution.py:152
  80.9 0.0 copy-start.3
  80.9 1.9 %copy-done.3 = bf16[1,1280,1280]{2,1,0:T(8,128)(2,1)S(1)} copy-done((bf16[1,1280,1280]{2,1,0:T(8,128)(2,1)S(1)}, bf16[1,1280,1280]{2,1,0:T(8,128)(2,1)}, u32[]{:S(2)}) %copy-start.3) | copy-done | bytes 3276824
  82.8 4.0 %expert.5 = bf16[128,2,640]{2,1,0:T(2,128)(2,1)S(1)} custom-call(bf16[128,2,640]{2,1,0:T(2,128)(2,1)} %collective-permute-done.rows_ref, bf16[1,1280,1280]{2,1,0:T(8,128)(2,1)S(1)} %copy-done, bf16[1,1280,1280]{2,1,0:T(8,128)(2,1)S(1)} %copy-done.3), custom_call_target="tpu_custom_call" | custom-call | flops 838860800 | bytes 6553600 | tf_op jit(solution)/shard_map/expert/pallas_call | solution.py:99
  86.8 0.4 collective-permute-start.1
  87.3 4.0 %expert.4 = bf16[128,2,640]{2,1,0:T(2,128)(2,1)S(1)} custom-call(bf16[128,2,640]{2,1,0:T(2,128)(2,1)} %all-to-all-done.rows_ref, bf16[1,1280,1280]{2,1,0:T(8,128)(2,1)S(1)} %copy-done, bf16[1,1280,1280]{2,1,0:T(8,128)(2,1)S(1)} %copy-done.3), custom_call_target="tpu_custom_call" | custom-call | flops 838860800 | bytes 6553600 | tf_op jit(solution)/shard_map/expert/pallas_call | solution.py:99
  91.3 6.4 %collective-permute-done.1 = bf16[128,2,640]{2,1,0:T(2,128)(2,1)S(1)} collective-permute-done((bf16[128,2,640]{2,1,0:T(2,128)(2,1)S(1)}, bf16[128,2,640]{2,1,0:T(2,128)(2,1)S(1)}, u32[]{:S(2)}, u32[]{:S(2)}) %collective-permute-start.1) | collective-permute-done | bytes 327712 | tf_op jit(solution)/shard_map/ppermute | solution.py:148
  97.7 1.1 add_convert_fusion.1
  98.8 12.8 %all-to-all-start.1 = ((bf16[128,2,640]{2,1,0:T(2,128)(2,1)}), bf16[128,2,640]{2,1,0:T(2,128)(2,1)S(1)}, u32[]{:S(2)}, u32[]{:S(2)}) async-start(bf16[128,2,640]{2,1,0:T(2,128)(2,1)} %add_convert_fusion.1), calls=%async_computation.1 | async-start | bytes 655360 | tf_op jit(solution)/shard_map/all_to_all | solution.py:152
  111.6 2.8 %mix.2.refs_0_ = bf16[2,256,1280]{2,1,0:T(8,128)(2,1)} custom-call(bf16[256,128]{1,0:T(8,128)(2,1)S(1)} %get-tuple-element.11.combine_ref, bf16[128,2,640]{2,1,0:T(2,128)(2,1)} %all-to-all-done.3.slots_ref), custom_call_target="tpu_custom_call" | custom-call | flops 83886080 | bytes 655360 | tf_op jit(solution)/shard_map/mix/pallas_call | solution.py:132
  114.5 13.1 %all-to-all-done.1.slots_ref = bf16[128,2,640]{2,1,0:T(2,128)(2,1)S(1)} async-done(((bf16[128,2,640]{2,1,0:T(2,128)(2,1)}), bf16[128,2,640]{2,1,0:T(2,128)(2,1)S(1)}, u32[]{:S(2)}, u32[]{:S(2)}) %all-to-all-start.1) | async-done | bytes 327712 | tf_op jit(solution)/shard_map/all_to_all | solution.py:152
  127.6 1.9 %mix.3 = bf16[2,256,1280]{2,1,0:T(8,128)(2,1)} custom-call(bf16[256,128]{1,0:T(8,128)(2,1)S(1)} %get-tuple-element.9.combine_ref, bf16[128,2,640]{2,1,0:T(2,128)(2,1)S(1)} %all-to-all-done.1.slots_ref, bf16[2,256,1280]{2,1,0:T(8,128)(2,1)} %mix.2.refs_0_), custom_call_target="tpu_custom_call", output_to_operand_aliasing={{}: (2, {})} | custom-call | flops 83886080 | bytes 655360 | tf_op jit(solution)/shard_map/mix/pallas_call | solution.py:132
  (8 shorter events, 0.0 us)
Async XLA Ops:
  1.4 1.3 %copy-start.4 = (bf16[2,256,1280]{2,1,0:T(8,128)(2,1)S(1)}, bf16[2,256,1280]{2,1,0:T(8,128)(2,1)}, u32[]{:S(2)}) copy-start(bf16[2,256,1280]{2,1,0:T(8,128)(2,1)} %tokens_ref.3) | copy-start | bytes 3932164
  2.7 1.0 copy-start.5
  3.6 43.2 %copy-start = (bf16[1,1280,1280]{2,1,0:T(8,128)(2,1)S(1)}, bf16[1,1280,1280]{2,1,0:T(8,128)(2,1)}, u32[]{:S(2)}) copy-start(bf16[1,1280,1280]{2,1,0:T(8,128)(2,1)} %up_ref.7) | copy-start | bytes 9830404
  35.5 11.3 %collective-permute-start.2 = (bf16[128,2,640]{2,1,0:T(2,128)(2,1)}, bf16[128,2,640]{2,1,0:T(2,128)(2,1)}, u32[]{:S(2)}, u32[]{:S(2)}) collective-permute-start(bf16[128,2,640]{2,1,0:T(2,128)(2,1)} %all_to_all.20.rows_ref), channel_id=1, source_target_pairs={{0,128},{128,0},{1,129},{129,1},{2,130},{130,2},{3,131},{131,3},{4... | collective-permute-start | bytes 983048 | tf_op jit(solution)/shard_map/ppermute | solution.py:148
  39.4 0.7 copy-start.6
  40.1 22.6 %all-to-all-start = ((bf16[128,2,640]{2,1,0:T(2,128)(2,1)}), bf16[128,2,640]{2,1,0:T(2,128)(2,1)}, u32[]{:S(2)}, u32[]{:S(2)}) async-start(bf16[128,2,640]{2,1,0:T(2,128)(2,1)} %copy-done.6), calls=%async_computation | async-start | bytes 655360 | tf_op jit(solution)/shard_map/all_to_all | solution.py:152
  46.9 1.9 %copy-start.1 = (bf16[1,1280,1280]{2,1,0:T(8,128)(2,1)S(1)}, bf16[1,1280,1280]{2,1,0:T(8,128)(2,1)}, u32[]{:S(2)}) copy-start(bf16[1,1280,1280]{2,1,0:T(8,128)(2,1)} %down_ref.7) | copy-start | bytes 9830404
  53.6 15.5 %collective-permute-start.3 = (bf16[128,2,640]{2,1,0:T(2,128)(2,1)}, bf16[128,2,640]{2,1,0:T(2,128)(2,1)}, u32[]{:S(2)}, u32[]{:S(2)}) collective-permute-start(bf16[128,2,640]{2,1,0:T(2,128)(2,1)} %expert.7), channel_id=1, source_target_pairs={{0,128},{128,0},{1,129},{129,1},{2,130},{130,2},{3,131},{131,3},{4... | collective-permute-start | bytes 983048 | tf_op jit(solution)/shard_map/ppermute | solution.py:148
  62.8 18.1 %collective-permute-start = (bf16[128,2,640]{2,1,0:T(2,128)(2,1)}, bf16[128,2,640]{2,1,0:T(2,128)(2,1)}, u32[]{:S(2)}, u32[]{:S(2)}) collective-permute-start(bf16[128,2,640]{2,1,0:T(2,128)(2,1)} %all-to-all-done.rows_ref), channel_id=1, source_target_pairs={{0,128},{128,0},{1,129},{129,1},{2,130},{130,2},{3,131},{131,3},{4... | collective-permute-start | bytes 983048 | tf_op jit(solution)/shard_map/ppermute | solution.py:148
  63.1 1.9 %copy-start.2 = (bf16[1,1280,1280]{2,1,0:T(8,128)(2,1)S(1)}, bf16[1,1280,1280]{2,1,0:T(8,128)(2,1)}, u32[]{:S(2)}) copy-start(bf16[1,1280,1280]{2,1,0:T(8,128)(2,1)} %down_ref.7) | copy-start | bytes 9830404
  71.1 27.7 %all-to-all-start.3 = ((bf16[128,2,640]{2,1,0:T(2,128)(2,1)}), bf16[128,2,640]{2,1,0:T(2,128)(2,1)}, u32[]{:S(2)}, u32[]{:S(2)}) async-start(bf16[128,2,640]{2,1,0:T(2,128)(2,1)} %add_convert_fusion), calls=%async_computation.3 | async-start | bytes 655360 | tf_op jit(solution)/shard_map/all_to_all | solution.py:152
  80.9 1.9 %copy-start.3 = (bf16[1,1280,1280]{2,1,0:T(8,128)(2,1)S(1)}, bf16[1,1280,1280]{2,1,0:T(8,128)(2,1)}, u32[]{:S(2)}) copy-start(bf16[1,1280,1280]{2,1,0:T(8,128)(2,1)} %down_ref.7) | copy-start | bytes 9830404
  86.8 10.9 %collective-permute-start.1 = (bf16[128,2,640]{2,1,0:T(2,128)(2,1)S(1)}, bf16[128,2,640]{2,1,0:T(2,128)(2,1)S(1)}, u32[]{:S(2)}, u32[]{:S(2)}) collective-permute-start(bf16[128,2,640]{2,1,0:T(2,128)(2,1)S(1)} %expert.5), channel_id=1, source_target_pairs={{0,128},{128,0},{1,129},{129,1},{2,130},{130,2},{3,131},{131,3},{4... | collective-permute-start | bytes 983048 | tf_op jit(solution)/shard_map/ppermute | solution.py:148
  98.8 28.8 %all-to-all-start.1 = ((bf16[128,2,640]{2,1,0:T(2,128)(2,1)}), bf16[128,2,640]{2,1,0:T(2,128)(2,1)S(1)}, u32[]{:S(2)}, u32[]{:S(2)}) async-start(bf16[128,2,640]{2,1,0:T(2,128)(2,1)} %add_convert_fusion.1), calls=%async_computation.1 | async-start | bytes 655360 | tf_op jit(solution)/shard_map/all_to_all | solution.py:152

commit v2 on v0

v2 whole, which is shorter than its diff:
```python
import jax
import jax.numpy as jnp
from jax import lax
from jax.experimental import pallas as pl
from jax.experimental.pallas import tpu as pltpu
from jax.sharding import Mesh
from jax.sharding import PartitionSpec as P

BF16 = jnp.bfloat16
F32 = jnp.float32
MIB = 1024 * 1024
AXES = ("dp", "x", "y_lo", "z", "core")
SIZES = (2, 4, 2, 8, 2)
INNER = 16
PLANE = ("x", "z", "core")
RING = ("dp", "y_lo")
RING_SIZE = 4
IMAGES = 2
VMEM = pl.BlockSpec(memory_space=pltpu.VMEM)
HBM = pl.BlockSpec(memory_space=pltpu.HBM)


def limit(mib):
    return pltpu.CompilerParams(vmem_limit_bytes=mib * MIB)


def column_slots(slots):
    column = lax.broadcasted_iota(jnp.int32, (1, IMAGES * slots), 1)
    slot = lax.broadcasted_iota(jnp.int32, (slots, IMAGES * slots), 0)
    group = (column >> 1) & 1
    place = column >> 2
    y_lo = (group + lax.axis_index("y_lo")) & 1
    wanted = (place >> 4) * (2 * INNER) + y_lo * INNER + (place & (INNER - 1))
    return (slot == wanted).astype(BF16)


def route_kernel(
    tokens_hbm, gain_hbm, params_hbm, scale_hbm, slots_ref, combine_ref,
    tokens_ref, gain_ref, params_ref, scale_ref, normed_ref, sems
):
    images, tokens, width = tokens_ref.shape
    copies = [
        pltpu.make_async_copy(params_hbm, params_ref, sems.at[0]),
        pltpu.make_async_copy(tokens_hbm.at[0], tokens_ref.at[0], sems.at[1]),
        pltpu.make_async_copy(gain_hbm, gain_ref, sems.at[2]),
        pltpu.make_async_copy(scale_hbm, scale_ref, sems.at[3]),
        pltpu.make_async_copy(tokens_hbm.at[1], tokens_ref.at[1], sems.at[4]),
    ]
    for copy in copies:
        copy.start()
    slots = params_ref.shape[1]
    columns = column_slots(slots)
    copies[0].wait()
    params = jnp.dot(params_ref[...], columns, preferred_element_type=F32)
    param_scale = lax.rsqrt(jnp.sum(params * params, axis=0, keepdims=True) + 1e-06)
    params = params.astype(BF16)
    copies[2].wait()
    copies[3].wait()
    gain = gain_ref[...].reshape(1, width)
    image_of = lax.broadcasted_iota(jnp.int32, (1, images * slots), 1) & 1
    dispatches = []
    block = 64
    for image in range(images):
        copies[1 if image == 0 else 4].wait()
        squares = []
        for at in range(0, tokens, block):
            floats = tokens_ref[image, at : at + block, :].astype(F32)
            centred = floats - jnp.mean(floats, axis=-1, keepdims=True)
            variance = jnp.mean(centred * centred, axis=-1, keepdims=True)
            normed = (centred * lax.rsqrt(variance + 1e-06) * gain).astype(BF16)
            normed_ref[image * tokens + at : image * tokens + at + block, :] = normed
            normed_f = normed.astype(F32)
            squares.append(jnp.sum(normed_f * normed_f, axis=-1, keepdims=True))
        token_scale = scale_ref[0] * lax.rsqrt(jnp.concatenate(squares, axis=0) + 1e-06)
        normed = normed_ref[image * tokens : (image + 1) * tokens, :]
        scores = jnp.dot(normed, params, preferred_element_type=F32)
        expo = jnp.exp(scores * token_scale * param_scale)
        expo = jnp.where(image_of == image, expo, 0.0)
        over_tokens = jnp.sum(expo, axis=0, keepdims=True)
        over_tokens = jnp.where(image_of == image, over_tokens, 1.0)
        dispatches.append((expo * (1.0 / over_tokens)).astype(BF16))
        combine_ref[image, :, :] = (expo * (1.0 / jnp.sum(expo, axis=1, keepdims=True))).astype(BF16)
    gathered = lax.dot_general(
        jnp.concatenate(dispatches, axis=0),
        normed_ref[...],
        (((0,), (0,)), ((), ())),
        preferred_element_type=F32,
    ).astype(BF16)
    slots_ref[...] = gathered.reshape(slots_ref.shape)


def route(tokens, norm_gain, slot_params, logit_scale):
    images, count, width = tokens.shape
    slots = slot_params.shape[1]
    return pl.pallas_call(
        route_kernel,
        in_specs=[HBM] * 4,
        out_specs=[VMEM] * 2,
        out_shape=[
            jax.ShapeDtypeStruct((slots // 2, 2, images, width), BF16),
            jax.ShapeDtypeStruct((images, count, images * slots), BF16),
        ],
        scratch_shapes=[
            pltpu.VMEM(tokens.shape, BF16),
            pltpu.VMEM(norm_gain.shape, F32),
            pltpu.VMEM(slot_params.shape, BF16),
            pltpu.SMEM(logit_scale.shape, F32),
            pltpu.VMEM((images * count, width), BF16),
            pltpu.SemaphoreType.DMA((5,)),
        ],
        compiler_params=limit(60),
        name="route",
    )(tokens, norm_gain, slot_params, logit_scale)


def expert_parts(rows, up_matrix, down_matrix):
    before = lax.dot_general(rows, up_matrix, (((1,), (1,)), ((), ())), preferred_element_type=F32)
    hidden = (before * (0.5 + 0.5 * lax.erf(before * (0.5**0.5)))).astype(BF16)
    return jnp.dot(hidden, down_matrix, preferred_element_type=F32).astype(BF16)


def first_expert_kernel(rows_ref, up_hbm, down_hbm, out_ref, up_ref, down_ref, sems):
    width = up_ref.shape[1]
    up_copy = pltpu.make_async_copy(up_hbm.at[0], up_ref, sems.at[0])
    down_copy = pltpu.make_async_copy(down_hbm.at[0], down_ref, sems.at[1])
    up_copy.start()
    down_copy.start()
    up_copy.wait()
    down_copy.wait()
    part = expert_parts(rows_ref[...].reshape(-1, width), up_ref[...], down_ref[...])
    out_ref[...] = part.reshape(out_ref.shape)


def first_expert(group, up_matrix, down_matrix):
    return pl.pallas_call(
        first_expert_kernel,
        in_specs=[VMEM, HBM, HBM],
        out_specs=[VMEM] * 3,
        out_shape=[
            jax.ShapeDtypeStruct(group.shape, BF16),
            jax.ShapeDtypeStruct(up_matrix.shape[1:], BF16),
            jax.ShapeDtypeStruct(down_matrix.shape[1:], BF16),
        ],
        scratch_shapes=[pltpu.SemaphoreType.DMA((2,))],
        compiler_params=limit(16),
        name="first_expert",
    )(group, up_matrix, down_matrix)


def expert_kernel(groups, *refs):
    up_ref, down_ref = refs[groups : groups + 2]
    outs = refs[groups + 2 :]
    width = up_ref.shape[1]
    flat = [ref[...].reshape(-1, width) for ref in refs[:groups]]
    count = flat[0].shape[0]
    rows = flat[0] if groups == 1 else jnp.concatenate(flat, axis=0)
    part = expert_parts(rows, up_ref[...], down_ref[...])
    for at, out_ref in enumerate(outs):
        out_ref[...] = part[at * count : (at + 1) * count].reshape(out_ref.shape)


def expert(groups, up_matrix, down_matrix):
    return pl.pallas_call(
        lambda *refs: expert_kernel(len(groups), *refs),
        in_specs=[VMEM] * (len(groups) + 2),
        out_specs=[VMEM] * len(groups),
        out_shape=[jax.ShapeDtypeStruct(group.shape, BF16) for group in groups],
        compiler_params=limit(16),
        name="expert",
    )(*groups, up_matrix, down_matrix)


def add_kernel(own_a_ref, own_b_ref, other_a_ref, other_b_ref, out_ref):
    for group, (a_ref, b_ref) in enumerate([(own_a_ref, own_b_ref), (other_a_ref, other_b_ref)]):
        out_ref[:, group, :, :] = (a_ref[...].astype(F32) + b_ref[...].astype(F32)).astype(BF16)


def add_parts(own, other):
    places, images, width = own[0].shape
    return pl.pallas_call(
        add_kernel,
        in_specs=[VMEM] * 4,
        out_specs=VMEM,
        out_shape=jax.ShapeDtypeStruct((places, 2, images, width), BF16),
        compiler_params=limit(16),
        name="add_parts",
    )(*own, *other)


def mix_kernel(combine_ref, slots_ref, out_hbm, out_ref, sems):
    images, _, columns = combine_ref.shape
    slots = slots_ref[...].reshape(columns, -1)
    copies = []
    for image in range(images):
        out_ref[image, :, :] = jnp.dot(combine_ref[image], slots, preferred_element_type=F32).astype(BF16)
        copies.append(pltpu.make_async_copy(out_ref.at[image], out_hbm.at[image], sems.at[image]))
        copies[-1].start()
    for copy in copies:
        copy.wait()


def mix(combine, slot_outputs):
    images, count, _ = combine.shape
    mixed = jax.ShapeDtypeStruct((images, count, slot_outputs.shape[-1]), BF16)
    return pl.pallas_call(
        mix_kernel,
        in_specs=[VMEM] * 2,
        out_specs=HBM,
        out_shape=mixed,
        scratch_shapes=[pltpu.VMEM(mixed.shape, BF16), pltpu.SemaphoreType.DMA((images,))],
        compiler_params=limit(16),
        name="mix",
    )(combine, slot_outputs)


def around(value, step):
    return lax.ppermute(value, RING, [(at, (at + step) % RING_SIZE) for at in range(RING_SIZE)])


def exchange(value):
    return lax.all_to_all(value, PLANE, split_axis=0, concat_axis=0, tiled=True)


def local(tokens, norm_gain, slot_params, logit_scale, expert_up, expert_down):
    slot_inputs, combine = route(tokens, norm_gain, slot_params, logit_scale)
    arrived = exchange(slot_inputs)
    own, other = arrived[:, 0], arrived[:, 1]
    below, above = around(other, 1), around(other, -1)
    kept, up_matrix, down_matrix = first_expert(own, expert_up, expert_down)
    own, kept = lax.optimization_barrier((own, kept))
    across = around(own, 2)
    below, above = expert([below, above], up_matrix, down_matrix)
    from_above, from_below = around(below, -1), around(above, 1)
    (across,) = expert([across], up_matrix, down_matrix)
    slot_outputs = add_parts((kept, around(across, 2)), (from_above, from_below))
    return mix(combine, exchange(slot_outputs))


def solution(mesh):
    fine = Mesh(mesh.devices.reshape(SIZES), AXES)
    expert_axes = AXES[1:]
    placed = (
        P(AXES, None, None),
        P(),
        P(),
        P(),
        P(expert_axes, "dp", None),
        P(expert_axes, "dp", None),
    )
    return jax.shard_map(
        local,
        mesh=fine,
        in_specs=placed,
        out_specs=P(AXES, None, None),
        check_vma=False,
    )
```

time: 180 us -> 107 us (0.59)
  waiting for transfers between devices: 54.9 us -> 19.1 us
  matrix products: 20.6 us -> 0 us
  between operations: 14.3 us -> 0.87 us
  Pallas kernels: 0 us -> 13.3 us
  blocking collectives: 71.6 us -> 60.9 us
  local copies, waits for them, and re-layouts: 12.8 us -> 2.38 us
  starting transfers between devices: 0.22 us -> 10.3 us
  other arithmetic: 5.37 us -> 0 us
    reduce_scatter x1 -> x0, waiting for transfers between devices: 29.4 us -> none  [local(): lax.psum_scatter(partial_out, 'dp', scatter_dimension=0, tiled=True)]
    all_gather x1 -> x0, waiting for transfers between devices: 25.5 us -> none  [local(): gathered = lax.all_gather(arrived, 'dp', axis=0, tiled=True)]
    dot_general x5 -> x0, matrix products: 20.6 us -> none  [the longest x1 9 us: local(): lax.dot_general(slot_rows, up_matrix, (((1,), (1,)), ((), ())), preferred...]
    ppermute x0 -> x6, waiting for transfers between devices: none -> 19.1 us  [around(): lax.ppermute(value, RING, [(at, (at + step) % RING_SIZE) for at in range(...]
    pallas_call x0 -> x6, Pallas kernels: none -> 13.3 us  [the longest x1 4.88 us: route(): pl.pallas_call(route_kernel, in_specs=[HBM] * 4, out_specs=[VMEM] * 2, ou...]
    all_to_all x2, blocking collectives: 71.6 us -> 60.9 us  [exchange(): return lax.all_to_all(value, PLANE, split_axis=0, concat_axis=0, tiled=True)]
    ppermute x0 -> x6, starting transfers between devices: none -> 10.3 us  [around(): lax.ppermute(value, RING, [(at, (at + step) % RING_SIZE) for at in range(...]
    reduce_sum x4 -> x0, other arithmetic: 5.33 us -> none  [the longest x1 1.8 us: normalize_tokens(): variance = jnp.mean(centred * centred, axis=-1, keepdims=True)]
  transfers between devices with their start and end apart: 2 -> 6, of which waited for: 2 -> 6; matrix products, arithmetic and copies ran while one was open for 0% -> 0% of each run, Pallas kernels for 0% -> 4%
where the time goes in v2:
time: 107 us
  blocking collectives  60.9 us (57%)
  waiting for transfers between devices  19.1 us (18%)
  Pallas kernels  13.3 us (12%)
  starting transfers between devices  10.3 us (10%)
  local copies, waits for them, and re-layouts  2.38 us (2%)
    all_to_all x2, blocking collectives, exchange(): return lax.all_to_all(value, PLANE, split_axis=0, concat_axis=0, tiled=True)  60.9 us
    ppermute x6, waiting for transfers between devices, around(): lax.ppermute(value, RING, [(at, (at + step) % RING_SIZE) for at in range(...  19.1 us
    ppermute x6, starting transfers between devices, around(): lax.ppermute(value, RING, [(at, (at + step) % RING_SIZE) for at in range(...  10.3 us
    pallas_call x1, Pallas kernels, route(): pl.pallas_call(route_kernel, in_specs=[HBM] * 4, out_specs=[VMEM] * 2, ou...  4.88 us
    pallas_call x2, Pallas kernels, expert(): pl.pallas_call(lambda *refs: expert_kernel(len(groups), *refs), in_specs=...  3.81 us
    pallas_call x1, Pallas kernels, first_expert(): pl.pallas_call(first_expert_kernel, in_specs=[VMEM, HBM, HBM], out_specs=...  2.56 us
  transfers between devices with their start and end apart: 6, of which 6 were waited for; matrix products, arithmetic and copies ran while one was open for 0% of the time, Pallas kernels for 4%

profile of v2, /device:TPU:1, one launch (start us, length us, event | category | flops | bytes accessed | tf_op | source)
XLA Modules:
  0.0 106.9 jit_solution(3341756738276935703)
XLA Ops:
  0.0 0.0 copy-start
  0.8 4.9 %route.1 = (bf16[64,2,2,1280]{3,2,1,0:T(2,128)(2,1)}, bf16[2,256,256]{2,1,0:T(8,128)(2,1)}) custom-call(bf16[2,256,1280]{2,1,0:T(8,128)(2,1)} %tokens_hbm.1, f32[1280]{0:T(1024)} %gain_hbm.1, bf16[1280,128]{1,0:T(8,128)(2,1)} %params_hbm.1, f32[1]{0:T(128)S(6)} %copy.12.scale_hbm), custom_call_target="tpu_custom_call" | custom-call | tf_op jit(solution)/shard_map/route/pallas_call | solution.py:95
  5.7 33.1 %all_to_all.10 = bf16[64,2,2,1280]{3,2,1,0:T(2,128)(2,1)S(1)} all-to-all(bf16[64,2,2,1280]{3,2,1,0:T(2,128)(2,1)} %get-tuple-element.15), channel_id=1, replica_groups=mesh['dp'=2,'x'=4,'y_lo'=2,'z'=8,'core'=2] {'x','z','core'}, dimensions={0} | all-to-all | bytes 1310720 | tf_op jit(solution)/shard_map/all_to_all | solution.py:221
  38.8 0.5 slice_bitcast_fusion
  39.3 0.0 copy-done
  39.3 0.0 copy-start.1
  39.3 1.9 %copy-done.1 = bf16[1,1280,1280]{2,1,0:T(8,128)(2,1)S(1)} copy-done((bf16[1,1280,1280]{2,1,0:T(8,128)(2,1)S(1)}, bf16[1,1280,1280]{2,1,0:T(8,128)(2,1)}, u32[]{:S(2)}) %copy-start.1) | copy-done | bytes 3276824
  41.2 2.6 %first_expert.1 = (bf16[64,2,1280]{2,1,0:T(2,128)(2,1)S(1)}, bf16[1280,1280]{1,0:T(8,128)(2,1)S(1)}, bf16[1280,1280]{1,0:T(8,128)(2,1)S(1)}) custom-call(bf16[64,2,1280]{2,1,0:T(2,128)(2,1)S(1)} %get-tuple-element.18.rows_ref, bf16[1,1280,1280]{2,1,0:T(8,128)(2,1)S(1)} %copy-done, bf16[1,1280,1280]{2,1,0:T(8,128)(2,1)S(1)} %copy-done.1), custom_call_target="tpu_custom_call" | custom-call | tf_op jit(solution)/shard_map/first_expert/pallas_call | solution.py:135
  43.8 3.0 %collective-permute-start = (bf16[64,2,1280]{2,1,0:T(2,128)(2,1)S(1)}, bf16[64,2,1280]{2,1,0:T(2,128)(2,1)S(1)}, u32[]{:S(2)}, u32[]{:S(2)}) collective-permute-start(bf16[64,2,1280]{2,1,0:T(2,128)(2,1)S(1)} %get-tuple-element.18.rows_ref), channel_id=1, source_target_pairs={{0,128},{16,144},{128,0},{144,16},{1,129},{17,145},{129,1},{145,17... | collective-permute-start | bytes 983048 | tf_op jit(solution)/shard_map/ppermute | solution.py:217
  46.8 0.8 collective-permute-start.3
  47.6 0.7 collective-permute-start.2
  48.3 6.2 %collective-permute-done.refs_0_ = bf16[64,2,1280]{2,1,0:T(2,128)(2,1)S(1)} collective-permute-done((bf16[64,2,1280]{2,1,0:T(2,128)(2,1)S(1)}, bf16[64,2,1280]{2,1,0:T(2,128)(2,1)S(1)}, u32[]{:S(2)}, u32[]{:S(2)}) %collective-permute-start) | collective-permute-done | bytes 327712 | tf_op jit(solution)/shard_map/ppermute | solution.py:217
  54.4 1.8 %expert.2 = bf16[64,2,1280]{2,1,0:T(2,128)(2,1)S(1)} custom-call(bf16[64,2,1280]{2,1,0:T(2,128)(2,1)S(1)} %collective-permute-done.refs_0_, bf16[1280,1280]{1,0:T(8,128)(2,1)S(1)} %get-tuple-element.19.refs_1_.refs_2_, bf16[1280,1280]{1,0:T(8,128)(2,1)S(1)} %get-tuple-element.20.refs_2_.refs_3_), custom_call_target="tpu_custom_call" | custom-call | tf_op jit(solution)/shard_map/expert/pallas_call | solution.py:163
  56.2 3.0 %collective-permute-start.1 = (bf16[64,2,1280]{2,1,0:T(2,128)(2,1)S(1)}, bf16[64,2,1280]{2,1,0:T(2,128)(2,1)S(1)}, u32[]{:S(2)}, u32[]{:S(2)}) collective-permute-start(bf16[64,2,1280]{2,1,0:T(2,128)(2,1)S(1)} %expert.2), channel_id=1, source_target_pairs={{0,128},{16,144},{128,0},{144,16},{1,129},{17,145},{129,1},{145,17... | collective-permute-start | bytes 983048 | tf_op jit(solution)/shard_map/ppermute | solution.py:217
  59.2 2.6 %collective-permute-done.3.refs_1_ = bf16[64,2,1280]{2,1,0:T(2,128)(2,1)S(1)} collective-permute-done((bf16[64,2,1280]{2,1,0:T(2,128)(2,1)S(1)}, bf16[64,2,1280]{2,1,0:T(2,128)(2,1)S(1)}, u32[]{:S(2)}, u32[]{:S(2)}) %collective-permute-start.3) | collective-permute-done | bytes 327712 | tf_op jit(solution)/shard_map/ppermute | solution.py:217
  61.8 0.8 collective-permute-done.2.refs_0_
  62.6 2.0 %expert.3 = (bf16[64,2,1280]{2,1,0:T(2,128)(2,1)S(1)}, bf16[64,2,1280]{2,1,0:T(2,128)(2,1)S(1)}) custom-call(bf16[64,2,1280]{2,1,0:T(2,128)(2,1)S(1)} %collective-permute-done.2.refs_0_, bf16[64,2,1280]{2,1,0:T(2,128)(2,1)S(1)} %collective-permute-done.3.refs_1_, bf16[1280,1280]{1,0:T(8,128)(2,1)S(1)} %get-tuple-element.19.refs_1_.refs_2_, ...), custom_call_target="tpu_custom_call" | custom-call | tf_op jit(solution)/shard_map/expert/pallas_call | solution.py:163
  64.6 0.0 copy-start.2
  64.6 2.8 %collective-permute-start.4 = (bf16[64,2,1280]{2,1,0:T(2,128)(2,1)S(1)}, bf16[64,2,1280]{2,1,0:T(2,128)(2,1)S(1)}, u32[]{:S(2)}, u32[]{:S(2)}) collective-permute-start(bf16[64,2,1280]{2,1,0:T(2,128)(2,1)S(1)} %get-tuple-element.21), channel_id=1, source_target_pairs={{0,144},{16,0},{128,16},{144,128},{1,145},{17,1},{129,17},{145,129... | collective-permute-start | bytes 983048 | tf_op jit(solution)/shard_map/ppermute | solution.py:217
  67.5 0.0 collective-permute-start.5
  67.5 1.0 collective-permute-done.1.own_b_ref
  68.5 7.4 %collective-permute-done.4.other_a_ref = bf16[64,2,1280]{2,1,0:T(2,128)(2,1)S(1)} collective-permute-done((bf16[64,2,1280]{2,1,0:T(2,128)(2,1)S(1)}, bf16[64,2,1280]{2,1,0:T(2,128)(2,1)S(1)}, u32[]{:S(2)}, u32[]{:S(2)}) %collective-permute-start.4) | collective-permute-done | bytes 327712 | tf_op jit(solution)/shard_map/ppermute | solution.py:217
  75.8 1.2 %collective-permute-done.5.other_b_ref = bf16[64,2,1280]{2,1,0:T(2,128)(2,1)S(1)} collective-permute-done((bf16[64,2,1280]{2,1,0:T(2,128)(2,1)S(1)}, bf16[64,2,1280]{2,1,0:T(2,128)(2,1)S(1)}, u32[]{:S(2)}, u32[]{:S(2)}) %collective-permute-start.5) | collective-permute-done | bytes 327712 | tf_op jit(solution)/shard_map/ppermute | solution.py:217
  77.0 0.6 add_parts.1
  77.6 27.8 %all_to_all.11.slots_ref = bf16[64,2,2,1280]{3,2,1,0:T(2,128)(2,1)S(1)} all-to-all(bf16[64,2,2,1280]{3,2,1,0:T(2,128)(2,1)S(1)} %add_parts.1), channel_id=1, replica_groups=mesh['dp'=2,'x'=4,'y_lo'=2,'z'=8,'core'=2] {'x','z','core'}, dimensions={0} | all-to-all | bytes 1310720 | tf_op jit(solution)/shard_map/all_to_all | solution.py:221
  105.4 0.0 copy-done.2
  105.4 1.5 %mix.1 = bf16[2,256,1280]{2,1,0:T(8,128)(2,1)} custom-call(bf16[2,256,256]{2,1,0:T(8,128)(2,1)S(1)} %copy-done.2, bf16[64,2,2,1280]{3,2,1,0:T(2,128)(2,1)S(1)} %all_to_all.11.slots_ref), custom_call_target="tpu_custom_call" | custom-call | tf_op jit(solution)/shard_map/mix/pallas_call | solution.py:205
Async XLA Ops:
  0.0 39.3 %copy-start = (bf16[1,1280,1280]{2,1,0:T(8,128)(2,1)S(1)}, bf16[1,1280,1280]{2,1,0:T(8,128)(2,1)}, u32[]{:S(2)}) copy-start(bf16[1,1280,1280]{2,1,0:T(8,128)(2,1)} %up_hbm.1) | copy-start | bytes 9830404
  39.3 1.9 %copy-start.1 = (bf16[1,1280,1280]{2,1,0:T(8,128)(2,1)S(1)}, bf16[1,1280,1280]{2,1,0:T(8,128)(2,1)}, u32[]{:S(2)}) copy-start(bf16[1,1280,1280]{2,1,0:T(8,128)(2,1)} %down_hbm.1) | copy-start | bytes 9830404
  43.8 10.6 %collective-permute-start = (bf16[64,2,1280]{2,1,0:T(2,128)(2,1)S(1)}, bf16[64,2,1280]{2,1,0:T(2,128)(2,1)S(1)}, u32[]{:S(2)}, u32[]{:S(2)}) collective-permute-start(bf16[64,2,1280]{2,1,0:T(2,128)(2,1)S(1)} %get-tuple-element.18.rows_ref), channel_id=1, source_target_pairs={{0,128},{16,144},{128,0},{144,16},{1,129},{17,145},{129,1},{145,17... | collective-permute-start | bytes 983048 | tf_op jit(solution)/shard_map/ppermute | solution.py:217
  46.8 15.0 %collective-permute-start.3 = (bf16[64,2,1280]{2,1,0:T(2,128)(2,1)S(1)}, bf16[64,2,1280]{2,1,0:T(2,128)(2,1)S(1)}, u32[]{:S(2)}, u32[]{:S(2)}) collective-permute-start(bf16[64,2,1280]{2,1,0:T(2,128)(2,1)S(1)} %get-tuple-element.23), channel_id=1, source_target_pairs={{0,144},{16,0},{128,16},{144,128},{1,145},{17,1},{129,17},{145,129... | collective-permute-start | bytes 983048 | tf_op jit(solution)/shard_map/ppermute | solution.py:217
  47.6 15.0 %collective-permute-start.2 = (bf16[64,2,1280]{2,1,0:T(2,128)(2,1)S(1)}, bf16[64,2,1280]{2,1,0:T(2,128)(2,1)S(1)}, u32[]{:S(2)}, u32[]{:S(2)}) collective-permute-start(bf16[64,2,1280]{2,1,0:T(2,128)(2,1)S(1)} %get-tuple-element.23), channel_id=1, source_target_pairs={{0,16},{16,128},{128,144},{144,0},{1,17},{17,129},{129,145},{145,1... | collective-permute-start | bytes 983048 | tf_op jit(solution)/shard_map/ppermute | solution.py:217
  56.2 12.3 %collective-permute-start.1 = (bf16[64,2,1280]{2,1,0:T(2,128)(2,1)S(1)}, bf16[64,2,1280]{2,1,0:T(2,128)(2,1)S(1)}, u32[]{:S(2)}, u32[]{:S(2)}) collective-permute-start(bf16[64,2,1280]{2,1,0:T(2,128)(2,1)S(1)} %expert.2), channel_id=1, source_target_pairs={{0,128},{16,144},{128,0},{144,16},{1,129},{17,145},{129,1},{145,17... | collective-permute-start | bytes 983048 | tf_op jit(solution)/shard_map/ppermute | solution.py:217
  64.6 40.8 %copy-start.2 = (bf16[2,256,256]{2,1,0:T(8,128)(2,1)S(1)}, bf16[2,256,256]{2,1,0:T(8,128)(2,1)}, u32[]{:S(2)}) copy-start(bf16[2,256,256]{2,1,0:T(8,128)(2,1)} %get-tuple-element.14.combine_ref) | copy-start | bytes 786436
  64.6 11.2 %collective-permute-start.4 = (bf16[64,2,1280]{2,1,0:T(2,128)(2,1)S(1)}, bf16[64,2,1280]{2,1,0:T(2,128)(2,1)S(1)}, u32[]{:S(2)}, u32[]{:S(2)}) collective-permute-start(bf16[64,2,1280]{2,1,0:T(2,128)(2,1)S(1)} %get-tuple-element.21), channel_id=1, source_target_pairs={{0,144},{16,0},{128,16},{144,128},{1,145},{17,1},{129,17},{145,129... | collective-permute-start | bytes 983048 | tf_op jit(solution)/shard_map/ppermute | solution.py:217
  67.5 9.5 %collective-permute-start.5 = (bf16[64,2,1280]{2,1,0:T(2,128)(2,1)S(1)}, bf16[64,2,1280]{2,1,0:T(2,128)(2,1)S(1)}, u32[]{:S(2)}, u32[]{:S(2)}) collective-permute-start(bf16[64,2,1280]{2,1,0:T(2,128)(2,1)S(1)} %get-tuple-element.22), channel_id=1, source_target_pairs={{0,16},{16,128},{128,144},{144,0},{1,17},{17,129},{129,145},{145,1... | collective-permute-start | bytes 983048 | tf_op jit(solution)/shard_map/ppermute | solution.py:217

commit v3 on v2

--- a/solution.py
+++ b/solution.py
@@ -14,7 +14,7 @@
 INNER = 16
 PLANE = ("x", "z", "core")
 RING = ("dp", "y_lo")
-RING_SIZE = 4
+EVEN, ODD, ACROSS = ((0, 1), (2, 3)), ((1, 2), (3, 0)), ((0, 2), (1, 3))
 IMAGES = 2
 VMEM = pl.BlockSpec(memory_space=pltpu.VMEM)
 HBM = pl.BlockSpec(memory_space=pltpu.HBM)
@@ -213,8 +213,8 @@
     )(combine, slot_outputs)
 
 
-def around(value, step):
-    return lax.ppermute(value, RING, [(at, (at + step) % RING_SIZE) for at in range(RING_SIZE)])
+def pairwise(value, pairs):
+    return lax.ppermute(value, RING, [(a, b) for a, b in pairs] + [(b, a) for a, b in pairs])
 
 
 def exchange(value):
@@ -225,14 +225,13 @@
     slot_inputs, combine = route(tokens, norm_gain, slot_params, logit_scale)
     arrived = exchange(slot_inputs)
     own, other = arrived[:, 0], arrived[:, 1]
-    below, above = around(other, 1), around(other, -1)
+    odd, even = pairwise(other, ODD), pairwise(other, EVEN)
+    across = pairwise(own, ACROSS)
     kept, up_matrix, down_matrix = first_expert(own, expert_up, expert_down)
-    own, kept = lax.optimization_barrier((own, kept))
-    across = around(own, 2)
-    below, above = expert([below, above], up_matrix, down_matrix)
-    from_above, from_below = around(below, -1), around(above, 1)
+    even, odd = expert([even, odd], up_matrix, down_matrix)
+    odd, even = pairwise(odd, ODD), pairwise(even, EVEN)
     (across,) = expert([across], up_matrix, down_matrix)
-    slot_outputs = add_parts((kept, around(across, 2)), (from_above, from_below))
+    slot_outputs = add_parts((kept, pairwise(across, ACROSS)), (even, odd))
     return mix(combine, exchange(slot_outputs))
 
 

time: 107 us -> 101 us (0.944)
  starting transfers between devices: 10.3 us -> 7.59 us
  waiting for transfers between devices: 19.1 us -> 16.7 us
    ppermute x6, starting transfers between devices: 10.3 us -> 7.59 us  [pairwise(): lax.ppermute(value, RING, [(a, b) for a, b in pairs] + [(b, a) for a, b i...]
    ppermute x6, waiting for transfers between devices: 19.1 us -> 16.7 us  [pairwise(): lax.ppermute(value, RING, [(a, b) for a, b in pairs] + [(b, a) for a, b i...]
  transfers between devices with their start and end apart: 6 -> 6, of which waited for: 6 -> 5; matrix products, arithmetic and copies ran while one was open for 0% -> 0% of each run, Pallas kernels for 4% -> 6%
where the time goes in v3:
time: 101 us
  blocking collectives  59.9 us (59%)
  waiting for transfers between devices  16.7 us (17%)
  Pallas kernels  13.3 us (13%)
  starting transfers between devices  7.59 us (8%)
  local copies, waits for them, and re-layouts  2.39 us (2%)
    all_to_all x2, blocking collectives, exchange(): return lax.all_to_all(value, PLANE, split_axis=0, concat_axis=0, tiled=True)  59.9 us
    ppermute x6, waiting for transfers between devices, pairwise(): lax.ppermute(value, RING, [(a, b) for a, b in pairs] + [(b, a) for a, b i...  16.7 us
    ppermute x6, starting transfers between devices, pairwise(): lax.ppermute(value, RING, [(a, b) for a, b in pairs] + [(b, a) for a, b i...  7.59 us
    pallas_call x1, Pallas kernels, route(): pl.pallas_call(route_kernel, in_specs=[HBM] * 4, out_specs=[VMEM] * 2, ou...  4.88 us
    pallas_call x2, Pallas kernels, expert(): pl.pallas_call(lambda *refs: expert_kernel(len(groups), *refs), in_specs=...  3.81 us
    pallas_call x1, Pallas kernels, first_expert(): pl.pallas_call(first_expert_kernel, in_specs=[VMEM, HBM, HBM], out_specs=...  2.56 us
  transfers between devices with their start and end apart: 6, of which 5 were waited for; matrix products, arithmetic and copies ran while one was open for 0% of the time, Pallas kernels for 6%

profile of v3, /device:TPU:1, one launch (start us, length us, event | category | flops | bytes accessed | tf_op | source)
XLA Modules:
  0.0 100.7 jit_solution(17034887080326684912)
XLA Ops:
  0.0 0.0 copy-start
  0.8 4.9 %route.1 = (bf16[64,2,2,1280]{3,2,1,0:T(2,128)(2,1)}, bf16[2,256,256]{2,1,0:T(8,128)(2,1)}) custom-call(bf16[2,256,1280]{2,1,0:T(8,128)(2,1)} %tokens_hbm.1, f32[1280]{0:T(1024)} %gain_hbm.1, bf16[1280,128]{1,0:T(8,128)(2,1)} %params_hbm.1, f32[1]{0:T(128)S(6)} %copy.12.scale_hbm), custom_call_target="tpu_custom_call" | custom-call | tf_op jit(solution)/shard_map/route/pallas_call | solution.py:95
  5.7 33.1 %all_to_all.10 = bf16[64,2,2,1280]{3,2,1,0:T(2,128)(2,1)S(1)} all-to-all(bf16[64,2,2,1280]{3,2,1,0:T(2,128)(2,1)} %get-tuple-element.13), channel_id=1, replica_groups=mesh['dp'=2,'x'=4,'y_lo'=2,'z'=8,'core'=2] {'x','z','core'}, dimensions={0} | all-to-all | bytes 1310720 | tf_op jit(solution)/shard_map/all_to_all | solution.py:221
  38.8 0.5 slice_bitcast_fusion
  39.3 2.8 %collective-permute-start.3 = (bf16[64,2,1280]{2,1,0:T(2,128)(2,1)S(1)}, bf16[64,2,1280]{2,1,0:T(2,128)(2,1)S(1)}, u32[]{:S(2)}, u32[]{:S(2)}) collective-permute-start(bf16[64,2,1280]{2,1,0:T(2,128)(2,1)S(1)} %get-tuple-element.19), channel_id=1, source_target_pairs={{16,128},{144,0},{128,16},{0,144},{17,129},{145,1},{129,17},{1,145... | collective-permute-start | bytes 983048 | tf_op jit(solution)/shard_map/ppermute | solution.py:217
  42.1 0.0 collective-permute-start.2
  42.1 1.3 %collective-permute-start = (bf16[64,2,1280]{2,1,0:T(2,128)(2,1)S(1)}, bf16[64,2,1280]{2,1,0:T(2,128)(2,1)S(1)}, u32[]{:S(2)}, u32[]{:S(2)}) collective-permute-start(bf16[64,2,1280]{2,1,0:T(2,128)(2,1)S(1)} %get-tuple-element.20.rows_ref), channel_id=1, source_target_pairs={{0,128},{16,144},{128,0},{144,16},{1,129},{17,145},{129,1},{145,17... | collective-permute-start | bytes 983048 | tf_op jit(solution)/shard_map/ppermute | solution.py:217
  43.4 0.0 copy-done
  43.4 0.0 copy-start.1
  43.4 1.9 %copy-done.1 = bf16[1,1280,1280]{2,1,0:T(8,128)(2,1)S(1)} copy-done((bf16[1,1280,1280]{2,1,0:T(8,128)(2,1)S(1)}, bf16[1,1280,1280]{2,1,0:T(8,128)(2,1)}, u32[]{:S(2)}) %copy-start.1) | copy-done | bytes 3276824
  45.3 2.6 %first_expert.1 = (bf16[64,2,1280]{2,1,0:T(2,128)(2,1)S(1)}, bf16[1280,1280]{1,0:T(8,128)(2,1)S(1)}, bf16[1280,1280]{1,0:T(8,128)(2,1)S(1)}) custom-call(bf16[64,2,1280]{2,1,0:T(2,128)(2,1)S(1)} %get-tuple-element.20.rows_ref, bf16[1,1280,1280]{2,1,0:T(8,128)(2,1)S(1)} %copy-done, bf16[1,1280,1280]{2,1,0:T(8,128)(2,1)S(1)} %copy-done.1), custom_call_target="tpu_custom_call" | custom-call | tf_op jit(solution)/shard_map/first_expert/pallas_call | solution.py:135
  47.9 1.8 %collective-permute-done.3.refs_1_ = bf16[64,2,1280]{2,1,0:T(2,128)(2,1)S(1)} collective-permute-done((bf16[64,2,1280]{2,1,0:T(2,128)(2,1)S(1)}, bf16[64,2,1280]{2,1,0:T(2,128)(2,1)S(1)}, u32[]{:S(2)}, u32[]{:S(2)}) %collective-permute-start.3) | collective-permute-done | bytes 327712 | tf_op jit(solution)/shard_map/ppermute | solution.py:217
  49.7 1.1 %collective-permute-done.2.refs_0_ = bf16[64,2,1280]{2,1,0:T(2,128)(2,1)S(1)} collective-permute-done((bf16[64,2,1280]{2,1,0:T(2,128)(2,1)S(1)}, bf16[64,2,1280]{2,1,0:T(2,128)(2,1)S(1)}, u32[]{:S(2)}, u32[]{:S(2)}) %collective-permute-start.2) | collective-permute-done | bytes 327712 | tf_op jit(solution)/shard_map/ppermute | solution.py:217
  50.8 2.0 %expert.3 = (bf16[64,2,1280]{2,1,0:T(2,128)(2,1)S(1)}, bf16[64,2,1280]{2,1,0:T(2,128)(2,1)S(1)}) custom-call(bf16[64,2,1280]{2,1,0:T(2,128)(2,1)S(1)} %collective-permute-done.2.refs_0_, bf16[64,2,1280]{2,1,0:T(2,128)(2,1)S(1)} %collective-permute-done.3.refs_1_, bf16[1280,1280]{1,0:T(8,128)(2,1)S(1)} %get-tuple-element.15.refs_1_.refs_2_, ...), custom_call_target="tpu_custom_call" | custom-call | tf_op jit(solution)/shard_map/expert/pallas_call | solution.py:163
  52.8 0.3 collective-permute-start.4
  53.1 1.5 %collective-permute-start.5 = (bf16[64,2,1280]{2,1,0:T(2,128)(2,1)S(1)}, bf16[64,2,1280]{2,1,0:T(2,128)(2,1)S(1)}, u32[]{:S(2)}, u32[]{:S(2)}) collective-permute-start(bf16[64,2,1280]{2,1,0:T(2,128)(2,1)S(1)} %get-tuple-element.18), channel_id=1, source_target_pairs={{16,128},{144,0},{128,16},{0,144},{17,129},{145,1},{129,17},{1,145... | collective-permute-start | bytes 983048 | tf_op jit(solution)/shard_map/ppermute | solution.py:217
  54.6 3.3 %collective-permute-done.refs_0_ = bf16[64,2,1280]{2,1,0:T(2,128)(2,1)S(1)} collective-permute-done((bf16[64,2,1280]{2,1,0:T(2,128)(2,1)S(1)}, bf16[64,2,1280]{2,1,0:T(2,128)(2,1)S(1)}, u32[]{:S(2)}, u32[]{:S(2)}) %collective-permute-start) | collective-permute-done | bytes 327712 | tf_op jit(solution)/shard_map/ppermute | solution.py:217
  57.8 1.8 %expert.2 = bf16[64,2,1280]{2,1,0:T(2,128)(2,1)S(1)} custom-call(bf16[64,2,1280]{2,1,0:T(2,128)(2,1)S(1)} %collective-permute-done.refs_0_, bf16[1280,1280]{1,0:T(8,128)(2,1)S(1)} %get-tuple-element.15.refs_1_.refs_2_, bf16[1280,1280]{1,0:T(8,128)(2,1)S(1)} %get-tuple-element.16.refs_2_.refs_3_), custom_call_target="tpu_custom_call" | custom-call | tf_op jit(solution)/shard_map/expert/pallas_call | solution.py:163
  59.6 0.0 copy-start.2
  59.6 1.8 %collective-permute-start.1 = (bf16[64,2,1280]{2,1,0:T(2,128)(2,1)S(1)}, bf16[64,2,1280]{2,1,0:T(2,128)(2,1)S(1)}, u32[]{:S(2)}, u32[]{:S(2)}) collective-permute-start(bf16[64,2,1280]{2,1,0:T(2,128)(2,1)S(1)} %expert.2), channel_id=1, source_target_pairs={{0,128},{16,144},{128,0},{144,16},{1,129},{17,145},{129,1},{145,17... | collective-permute-start | bytes 983048 | tf_op jit(solution)/shard_map/ppermute | solution.py:217
  61.4 3.5 %collective-permute-done.4.other_a_ref = bf16[64,2,1280]{2,1,0:T(2,128)(2,1)S(1)} collective-permute-done((bf16[64,2,1280]{2,1,0:T(2,128)(2,1)S(1)}, bf16[64,2,1280]{2,1,0:T(2,128)(2,1)S(1)}, u32[]{:S(2)}, u32[]{:S(2)}) %collective-permute-start.4) | collective-permute-done | bytes 327712 | tf_op jit(solution)/shard_map/ppermute | solution.py:217
  64.9 0.0 collective-permute-done.5.other_b_ref
  64.9 7.0 %collective-permute-done.1.own_b_ref = bf16[64,2,1280]{2,1,0:T(2,128)(2,1)S(1)} collective-permute-done((bf16[64,2,1280]{2,1,0:T(2,128)(2,1)S(1)}, bf16[64,2,1280]{2,1,0:T(2,128)(2,1)S(1)}, u32[]{:S(2)}, u32[]{:S(2)}) %collective-permute-start.1) | collective-permute-done | bytes 327712 | tf_op jit(solution)/shard_map/ppermute | solution.py:217
  71.9 0.6 add_parts.1
  72.5 26.8 %all_to_all.11.slots_ref = bf16[64,2,2,1280]{3,2,1,0:T(2,128)(2,1)S(1)} all-to-all(bf16[64,2,2,1280]{3,2,1,0:T(2,128)(2,1)S(1)} %add_parts.1), channel_id=1, replica_groups=mesh['dp'=2,'x'=4,'y_lo'=2,'z'=8,'core'=2] {'x','z','core'}, dimensions={0} | all-to-all | bytes 1310720 | tf_op jit(solution)/shard_map/all_to_all | solution.py:221
  99.3 0.0 copy-done.2
  99.3 1.5 %mix.1 = bf16[2,256,1280]{2,1,0:T(8,128)(2,1)} custom-call(bf16[2,256,256]{2,1,0:T(8,128)(2,1)S(1)} %copy-done.2, bf16[64,2,2,1280]{3,2,1,0:T(2,128)(2,1)S(1)} %all_to_all.11.slots_ref), custom_call_target="tpu_custom_call" | custom-call | tf_op jit(solution)/shard_map/mix/pallas_call | solution.py:205
Async XLA Ops:
  0.0 43.4 %copy-start = (bf16[1,1280,1280]{2,1,0:T(8,128)(2,1)S(1)}, bf16[1,1280,1280]{2,1,0:T(8,128)(2,1)}, u32[]{:S(2)}) copy-start(bf16[1,1280,1280]{2,1,0:T(8,128)(2,1)} %up_hbm.1) | copy-start | bytes 9830404
  39.3 10.4 %collective-permute-start.3 = (bf16[64,2,1280]{2,1,0:T(2,128)(2,1)S(1)}, bf16[64,2,1280]{2,1,0:T(2,128)(2,1)S(1)}, u32[]{:S(2)}, u32[]{:S(2)}) collective-permute-start(bf16[64,2,1280]{2,1,0:T(2,128)(2,1)S(1)} %get-tuple-element.19), channel_id=1, source_target_pairs={{16,128},{144,0},{128,16},{0,144},{17,129},{145,1},{129,17},{1,145... | collective-permute-start | bytes 983048 | tf_op jit(solution)/shard_map/ppermute | solution.py:217
  42.1 8.7 %collective-permute-start.2 = (bf16[64,2,1280]{2,1,0:T(2,128)(2,1)S(1)}, bf16[64,2,1280]{2,1,0:T(2,128)(2,1)S(1)}, u32[]{:S(2)}, u32[]{:S(2)}) collective-permute-start(bf16[64,2,1280]{2,1,0:T(2,128)(2,1)S(1)} %get-tuple-element.19), channel_id=1, source_target_pairs={{0,16},{128,144},{16,0},{144,128},{1,17},{129,145},{17,1},{145,129... | collective-permute-start | bytes 983048 | tf_op jit(solution)/shard_map/ppermute | solution.py:217
  42.1 15.7 %collective-permute-start = (bf16[64,2,1280]{2,1,0:T(2,128)(2,1)S(1)}, bf16[64,2,1280]{2,1,0:T(2,128)(2,1)S(1)}, u32[]{:S(2)}, u32[]{:S(2)}) collective-permute-start(bf16[64,2,1280]{2,1,0:T(2,128)(2,1)S(1)} %get-tuple-element.20.rows_ref), channel_id=1, source_target_pairs={{0,128},{16,144},{128,0},{144,16},{1,129},{17,145},{129,1},{145,17... | collective-permute-start | bytes 983048 | tf_op jit(solution)/shard_map/ppermute | solution.py:217
  43.4 1.9 %copy-start.1 = (bf16[1,1280,1280]{2,1,0:T(8,128)(2,1)S(1)}, bf16[1,1280,1280]{2,1,0:T(8,128)(2,1)}, u32[]{:S(2)}) copy-start(bf16[1,1280,1280]{2,1,0:T(8,128)(2,1)} %down_hbm.1) | copy-start | bytes 9830404
  52.8 12.0 %collective-permute-start.4 = (bf16[64,2,1280]{2,1,0:T(2,128)(2,1)S(1)}, bf16[64,2,1280]{2,1,0:T(2,128)(2,1)S(1)}, u32[]{:S(2)}, u32[]{:S(2)}) collective-permute-start(bf16[64,2,1280]{2,1,0:T(2,128)(2,1)S(1)} %get-tuple-element.17), channel_id=1, source_target_pairs={{0,16},{128,144},{16,0},{144,128},{1,17},{129,145},{17,1},{145,129... | collective-permute-start | bytes 983048 | tf_op jit(solution)/shard_map/ppermute | solution.py:217
  53.1 11.8 %collective-permute-start.5 = (bf16[64,2,1280]{2,1,0:T(2,128)(2,1)S(1)}, bf16[64,2,1280]{2,1,0:T(2,128)(2,1)S(1)}, u32[]{:S(2)}, u32[]{:S(2)}) collective-permute-start(bf16[64,2,1280]{2,1,0:T(2,128)(2,1)S(1)} %get-tuple-element.18), channel_id=1, source_target_pairs={{16,128},{144,0},{128,16},{0,144},{17,129},{145,1},{129,17},{1,145... | collective-permute-start | bytes 983048 | tf_op jit(solution)/shard_map/ppermute | solution.py:217
  59.6 39.7 %copy-start.2 = (bf16[2,256,256]{2,1,0:T(8,128)(2,1)S(1)}, bf16[2,256,256]{2,1,0:T(8,128)(2,1)}, u32[]{:S(2)}) copy-start(bf16[2,256,256]{2,1,0:T(8,128)(2,1)} %get-tuple-element.12.combine_ref) | copy-start | bytes 786436
  59.6 12.3 %collective-permute-start.1 = (bf16[64,2,1280]{2,1,0:T(2,128)(2,1)S(1)}, bf16[64,2,1280]{2,1,0:T(2,128)(2,1)S(1)}, u32[]{:S(2)}, u32[]{:S(2)}) collective-permute-start(bf16[64,2,1280]{2,1,0:T(2,128)(2,1)S(1)} %expert.2), channel_id=1, source_target_pairs={{0,128},{16,144},{128,0},{144,16},{1,129},{17,145},{129,1},{145,17... | collective-permute-start | bytes 983048 | tf_op jit(solution)/shard_map/ppermute | solution.py:217

commit v4 on v3

--- a/solution.py
+++ b/solution.py
@@ -35,8 +35,8 @@
 
 
 def route_kernel(
-    tokens_hbm, gain_hbm, params_hbm, scale_hbm, slots_ref, combine_ref,
-    tokens_ref, gain_ref, params_ref, scale_ref, normed_ref, sems
+    tokens_hbm, gain_hbm, params_hbm, scale_hbm, slots_hbm, combine_hbm,
+    tokens_ref, gain_ref, params_ref, scale_ref, normed_ref, slots_ref, combine_ref, sems
 ):
     images, tokens, width = tokens_ref.shape
     copies = [
@@ -80,13 +80,23 @@
         over_tokens = jnp.where(image_of == image, over_tokens, 1.0)
         dispatches.append((expo * (1.0 / over_tokens)).astype(BF16))
         combine_ref[image, :, :] = (expo * (1.0 / jnp.sum(expo, axis=1, keepdims=True))).astype(BF16)
-    gathered = lax.dot_general(
-        jnp.concatenate(dispatches, axis=0),
-        normed_ref[...],
-        (((0,), (0,)), ((), ())),
-        preferred_element_type=F32,
-    ).astype(BF16)
-    slots_ref[...] = gathered.reshape(slots_ref.shape)
+        copies.append(pltpu.make_async_copy(combine_ref.at[image], combine_hbm.at[image], sems.at[5 + image]))
+        copies[-1].start()
+    dispatch = jnp.concatenate(dispatches, axis=0)
+    places = slots_ref.shape[0] // 2
+    for half in range(2):
+        part = slice(half * places, (half + 1) * places)
+        gathered = lax.dot_general(
+            dispatch[:, half * slots : (half + 1) * slots],
+            normed_ref[...],
+            (((0,), (0,)), ((), ())),
+            preferred_element_type=F32,
+        ).astype(BF16)
+        slots_ref[part] = gathered.reshape(places, *slots_ref.shape[1:])
+        copies.append(pltpu.make_async_copy(slots_ref.at[part], slots_hbm.at[part], sems.at[7 + half]))
+        copies[-1].start()
+    for copy in copies[5:]:
+        copy.wait()
 
 
 def route(tokens, norm_gain, slot_params, logit_scale):
@@ -95,7 +105,7 @@
     return pl.pallas_call(
         route_kernel,
         in_specs=[HBM] * 4,
-        out_specs=[VMEM] * 2,
+        out_specs=[HBM] * 2,
         out_shape=[
             jax.ShapeDtypeStruct((slots // 2, 2, images, width), BF16),
             jax.ShapeDtypeStruct((images, count, images * slots), BF16),
@@ -106,7 +116,9 @@
             pltpu.VMEM(slot_params.shape, BF16),
             pltpu.SMEM(logit_scale.shape, F32),
             pltpu.VMEM((images * count, width), BF16),
-            pltpu.SemaphoreType.DMA((5,)),
+            pltpu.VMEM((slots // 2, 2, images, width), BF16),
+            pltpu.VMEM((images, count, images * slots), BF16),
+            pltpu.SemaphoreType.DMA((9,)),
         ],
         compiler_params=limit(60),
         name="route",
@@ -114,21 +126,21 @@
 
 
 def expert_parts(rows, up_matrix, down_matrix):
-    before = lax.dot_general(rows, up_matrix, (((1,), (1,)), ((), ())), preferred_element_type=F32)
+    before = jnp.dot(rows, up_matrix, preferred_element_type=F32)
     hidden = (before * (0.5 + 0.5 * lax.erf(before * (0.5**0.5)))).astype(BF16)
     return jnp.dot(hidden, down_matrix, preferred_element_type=F32).astype(BF16)
 
 
 def first_expert_kernel(rows_ref, up_hbm, down_hbm, out_ref, up_ref, down_ref, sems):
-    width = up_ref.shape[1]
     up_copy = pltpu.make_async_copy(up_hbm.at[0], up_ref, sems.at[0])
     down_copy = pltpu.make_async_copy(down_hbm.at[0], down_ref, sems.at[1])
     up_copy.start()
     down_copy.start()
     up_copy.wait()
     down_copy.wait()
-    part = expert_parts(rows_ref[...].reshape(-1, width), up_ref[...], down_ref[...])
-    out_ref[...] = part.reshape(out_ref.shape)
+    up_ref[...] = up_ref[...].T
+    part = expert_parts(rows_ref[...], up_ref[...], down_ref[...])
+    out_ref[...] = part
 
 
 def first_expert(group, up_matrix, down_matrix):
@@ -138,7 +150,7 @@
         out_specs=[VMEM] * 3,
         out_shape=[
             jax.ShapeDtypeStruct(group.shape, BF16),
-            jax.ShapeDtypeStruct(up_matrix.shape[1:], BF16),
+            jax.ShapeDtypeStruct(up_matrix.shape[:0:-1], BF16),
             jax.ShapeDtypeStruct(down_matrix.shape[1:], BF16),
         ],
         scratch_shapes=[pltpu.SemaphoreType.DMA((2,))],
@@ -150,13 +162,12 @@
 def expert_kernel(groups, *refs):
     up_ref, down_ref = refs[groups : groups + 2]
     outs = refs[groups + 2 :]
-    width = up_ref.shape[1]
-    flat = [ref[...].reshape(-1, width) for ref in refs[:groups]]
+    flat = [ref[...] for ref in refs[:groups]]
     count = flat[0].shape[0]
     rows = flat[0] if groups == 1 else jnp.concatenate(flat, axis=0)
     part = expert_parts(rows, up_ref[...], down_ref[...])
     for at, out_ref in enumerate(outs):
-        out_ref[...] = part[at * count : (at + 1) * count].reshape(out_ref.shape)
+        out_ref[...] = part[at * count : (at + 1) * count]
 
 
 def expert(groups, up_matrix, down_matrix):
@@ -170,18 +181,38 @@
     )(*groups, up_matrix, down_matrix)
 
 
+def split_kernel(arrived_ref, own_ref, other_ref):
+    own_ref[...] = arrived_ref[:, 0, :, :].reshape(own_ref.shape)
+    other_ref[...] = arrived_ref[:, 1, :, :].reshape(other_ref.shape)
+
+
+def split(arrived):
+    places, _, images, width = arrived.shape
+    group = jax.ShapeDtypeStruct((places * images, width), BF16)
+    return pl.pallas_call(
+        split_kernel,
+        in_specs=[VMEM],
+        out_specs=[VMEM] * 2,
+        out_shape=[group, group],
+        compiler_params=limit(16),
+        name="split",
+    )(arrived)
+
+
 def add_kernel(own_a_ref, own_b_ref, other_a_ref, other_b_ref, out_ref):
+    places, _, images, width = out_ref.shape
     for group, (a_ref, b_ref) in enumerate([(own_a_ref, own_b_ref), (other_a_ref, other_b_ref)]):
-        out_ref[:, group, :, :] = (a_ref[...].astype(F32) + b_ref[...].astype(F32)).astype(BF16)
+        total = (a_ref[...].astype(F32) + b_ref[...].astype(F32)).astype(BF16)
+        out_ref[:, group, :, :] = total.reshape(places, images, width)
 
 
 def add_parts(own, other):
-    places, images, width = own[0].shape
+    rows, width = own[0].shape
     return pl.pallas_call(
         add_kernel,
         in_specs=[VMEM] * 4,
         out_specs=VMEM,
-        out_shape=jax.ShapeDtypeStruct((places, 2, images, width), BF16),
+        out_shape=jax.ShapeDtypeStruct((rows // IMAGES, 2, IMAGES, width), BF16),
         compiler_params=limit(16),
         name="add_parts",
     )(*own, *other)
@@ -191,10 +222,16 @@
     images, _, columns = combine_ref.shape
     slots = slots_ref[...].reshape(columns, -1)
     copies = []
+    half = combine_ref.shape[1] // 2
     for image in range(images):
-        out_ref[image, :, :] = jnp.dot(combine_ref[image], slots, preferred_element_type=F32).astype(BF16)
-        copies.append(pltpu.make_async_copy(out_ref.at[image], out_hbm.at[image], sems.at[image]))
-        copies[-1].start()
+        for at in range(2):
+            part = slice(at * half, (at + 1) * half)
+            mixed = jnp.dot(combine_ref[image, part, :], slots, preferred_element_type=F32)
+            out_ref[image, part, :] = mixed.astype(BF16)
+            copies.append(
+                pltpu.make_async_copy(out_ref.at[image, part], out_hbm.at[image, part], sems.at[image, at])
+            )
+            copies[-1].start()
     for copy in copies:
         copy.wait()
 
@@ -207,7 +244,7 @@
         in_specs=[VMEM] * 2,
         out_specs=HBM,
         out_shape=mixed,
-        scratch_shapes=[pltpu.VMEM(mixed.shape, BF16), pltpu.SemaphoreType.DMA((images,))],
+        scratch_shapes=[pltpu.VMEM(mixed.shape, BF16), pltpu.SemaphoreType.DMA((images, 2))],
         compiler_params=limit(16),
         name="mix",
     )(combine, slot_outputs)
@@ -224,7 +261,7 @@
 def local(tokens, norm_gain, slot_params, logit_scale, expert_up, expert_down):
     slot_inputs, combine = route(tokens, norm_gain, slot_params, logit_scale)
     arrived = exchange(slot_inputs)
-    own, other = arrived[:, 0], arrived[:, 1]
+    own, other = split(arrived)
     odd, even = pairwise(other, ODD), pairwise(other, EVEN)
     across = pairwise(own, ACROSS)
     kept, up_matrix, down_matrix = first_expert(own, expert_up, expert_down)

time: 101 us -> 100 us (0.990)
  Pallas kernels: 13.3 us -> 12.1 us
    pallas_call x1 -> x2, Pallas kernels: 4.88 us -> 4.87 us  [the longest x1 4.78 us: route(): pl.pallas_call(route_kernel, in_specs=[HBM] * 4, out_specs=[HBM] * 2, out...]
where the time goes in v4:
time: 100 us; the launch traced here: 99.8 us
  blocking collectives  59.9 us (60%)
  waiting for transfers between devices  17.5 us (18%)
  Pallas kernels  12.1 us (12%)
  starting transfers between devices  7.58 us (8%)
  local copies, waits for them, and re-layouts  1.93 us (2%)
    all_to_all x2, blocking collectives, exchange(): return lax.all_to_all(value, PLANE, split_axis=0, concat_axis=0, tiled=True)  59.9 us
    ppermute x6, waiting for transfers between devices, pairwise(): lax.ppermute(value, RING, [(a, b) for a, b in pairs] + [(b, a) for a, b i...  17.5 us
    ppermute x6, starting transfers between devices, pairwise(): lax.ppermute(value, RING, [(a, b) for a, b in pairs] + [(b, a) for a, b i...  7.58 us
    pallas_call x1, Pallas kernels, route(): pl.pallas_call(route_kernel, in_specs=[HBM] * 4, out_specs=[HBM] * 2, out...  4.78 us
    pallas_call x2, Pallas kernels, expert(): pl.pallas_call(lambda *refs: expert_kernel(len(groups), *refs), in_specs=...  3.16 us
    pallas_call x1, Pallas kernels, first_expert(): pl.pallas_call(first_expert_kernel, in_specs=[VMEM, HBM, HBM], out_specs=...  2.39 us
  transfers between devices with their start and end apart: 6, of which 5 were waited for; matrix products, arithmetic and copies ran while one was open for 0% of the time, Pallas kernels for 6%

profile of v4, /device:TPU:1, one launch (start us, length us, event | category | flops | bytes accessed | tf_op | source)
XLA Modules:
  0.0 99.8 jit_solution(1406147469125062371)
XLA Ops:
  0.0 0.0 copy-start
  0.8 4.8 %route.1 = (bf16[64,2,2,1280]{3,2,1,0:T(2,128)(2,1)}, bf16[2,256,256]{2,1,0:T(8,128)(2,1)}) custom-call(bf16[2,256,1280]{2,1,0:T(8,128)(2,1)} %tokens_hbm.1, f32[1280]{0:T(1024)} %gain_hbm.1, bf16[1280,128]{1,0:T(8,128)(2,1)} %params_hbm.1, f32[1]{0:T(128)S(6)} %copy.7.scale_hbm), custom_call_target="tpu_custom_call" | custom-call | tf_op jit(solution)/shard_map/route/pallas_call | solution.py:105
  5.6 33.1 %all_to_all.10.arrived_ref = bf16[64,2,2,1280]{3,2,1,0:T(2,128)(2,1)S(1)} all-to-all(bf16[64,2,2,1280]{3,2,1,0:T(2,128)(2,1)} %get-tuple-element.15), channel_id=1, replica_groups=mesh['dp'=2,'x'=4,'y_lo'=2,'z'=8,'core'=2] {'x','z','core'}, dimensions={0} | all-to-all | bytes 1310720 | tf_op jit(solution)/shard_map/all_to_all | solution.py:258
  38.7 0.1 split.1
  38.8 2.8 %collective-permute-start.3 = (bf16[128,1280]{1,0:T(8,128)(2,1)S(1)}, bf16[128,1280]{1,0:T(8,128)(2,1)S(1)}, u32[]{:S(2)}, u32[]{:S(2)}) collective-permute-start(bf16[128,1280]{1,0:T(8,128)(2,1)S(1)} %get-tuple-element.20), channel_id=1, source_target_pairs={{16,128},{144,0},{128,16},{0,144},{17,129},{145,1},{129,17},{1,145... | collective-permute-start | bytes 983048 | tf_op jit(solution)/shard_map/ppermute | solution.py:254
  41.6 0.0 collective-permute-start.2
  41.6 1.3 %collective-permute-start = (bf16[128,1280]{1,0:T(8,128)(2,1)S(1)}, bf16[128,1280]{1,0:T(8,128)(2,1)S(1)}, u32[]{:S(2)}, u32[]{:S(2)}) collective-permute-start(bf16[128,1280]{1,0:T(8,128)(2,1)S(1)} %get-tuple-element.16.rows_ref), channel_id=1, source_target_pairs={{0,128},{16,144},{128,0},{144,16},{1,129},{17,145},{129,1},{145,17... | collective-permute-start | bytes 983048 | tf_op jit(solution)/shard_map/ppermute | solution.py:254
  42.9 0.0 copy-done
  42.9 0.0 copy-start.1
  42.9 1.9 %copy-done.1 = bf16[1,1280,1280]{2,1,0:T(8,128)(2,1)S(1)} copy-done((bf16[1,1280,1280]{2,1,0:T(8,128)(2,1)S(1)}, bf16[1,1280,1280]{2,1,0:T(8,128)(2,1)}, u32[]{:S(2)}) %copy-start.1) | copy-done | bytes 3276824
  44.9 2.4 %first_expert.1 = (bf16[128,1280]{1,0:T(8,128)(2,1)S(1)}, bf16[1280,1280]{1,0:T(8,128)(2,1)S(1)}, bf16[1280,1280]{1,0:T(8,128)(2,1)S(1)}) custom-call(bf16[128,1280]{1,0:T(8,128)(2,1)S(1)} %get-tuple-element.16.rows_ref, bf16[1,1280,1280]{2,1,0:T(8,128)(2,1)S(1)} %copy-done, bf16[1,1280,1280]{2,1,0:T(8,128)(2,1)S(1)} %copy-done.1), custom_call_target="tpu_custom_call" | custom-call | tf_op jit(solution)/shard_map/first_expert/pallas_call | solution.py:147
  47.3 2.0 %collective-permute-done.3.refs_1_ = bf16[128,1280]{1,0:T(8,128)(2,1)S(1)} collective-permute-done((bf16[128,1280]{1,0:T(8,128)(2,1)S(1)}, bf16[128,1280]{1,0:T(8,128)(2,1)S(1)}, u32[]{:S(2)}, u32[]{:S(2)}) %collective-permute-start.3) | collective-permute-done | bytes 327712 | tf_op jit(solution)/shard_map/ppermute | solution.py:254
  49.3 1.1 %collective-permute-done.2.refs_0_ = bf16[128,1280]{1,0:T(8,128)(2,1)S(1)} collective-permute-done((bf16[128,1280]{1,0:T(8,128)(2,1)S(1)}, bf16[128,1280]{1,0:T(8,128)(2,1)S(1)}, u32[]{:S(2)}, u32[]{:S(2)}) %collective-permute-start.2) | collective-permute-done | bytes 327712 | tf_op jit(solution)/shard_map/ppermute | solution.py:254
  50.3 2.0 %expert.3 = (bf16[128,1280]{1,0:T(8,128)(2,1)S(1)}, bf16[128,1280]{1,0:T(8,128)(2,1)S(1)}) custom-call(bf16[128,1280]{1,0:T(8,128)(2,1)S(1)} %collective-permute-done.2.refs_0_, bf16[128,1280]{1,0:T(8,128)(2,1)S(1)} %collective-permute-done.3.refs_1_, bf16[1280,1280]{1,0:T(8,128)(2,1)S(1)} %get-tuple-element.18.refs_1_.refs_2_, ...), custom_call_target="tpu_custom_call" | custom-call | tf_op jit(solution)/shard_map/expert/pallas_call | solution.py:174
  52.3 0.3 collective-permute-start.4
  52.6 1.5 %collective-permute-start.5 = (bf16[128,1280]{1,0:T(8,128)(2,1)S(1)}, bf16[128,1280]{1,0:T(8,128)(2,1)S(1)}, u32[]{:S(2)}, u32[]{:S(2)}) collective-permute-start(bf16[128,1280]{1,0:T(8,128)(2,1)S(1)} %get-tuple-element.22), channel_id=1, source_target_pairs={{16,128},{144,0},{128,16},{0,144},{17,129},{145,1},{129,17},{1,145... | collective-permute-start | bytes 983048 | tf_op jit(solution)/shard_map/ppermute | solution.py:254
  54.1 3.3 %collective-permute-done.refs_0_ = bf16[128,1280]{1,0:T(8,128)(2,1)S(1)} collective-permute-done((bf16[128,1280]{1,0:T(8,128)(2,1)S(1)}, bf16[128,1280]{1,0:T(8,128)(2,1)S(1)}, u32[]{:S(2)}, u32[]{:S(2)}) %collective-permute-start) | collective-permute-done | bytes 327712 | tf_op jit(solution)/shard_map/ppermute | solution.py:254
  57.4 1.2 %expert.2 = bf16[128,1280]{1,0:T(8,128)(2,1)S(1)} custom-call(bf16[128,1280]{1,0:T(8,128)(2,1)S(1)} %collective-permute-done.refs_0_, bf16[1280,1280]{1,0:T(8,128)(2,1)S(1)} %get-tuple-element.18.refs_1_.refs_2_, bf16[1280,1280]{1,0:T(8,128)(2,1)S(1)} %get-tuple-element.19.refs_2_.refs_3_), custom_call_target="tpu_custom_call" | custom-call | tf_op jit(solution)/shard_map/expert/pallas_call | solution.py:174
  58.5 0.0 copy-start.2
  58.5 1.8 %collective-permute-start.1 = (bf16[128,1280]{1,0:T(8,128)(2,1)S(1)}, bf16[128,1280]{1,0:T(8,128)(2,1)S(1)}, u32[]{:S(2)}, u32[]{:S(2)}) collective-permute-start(bf16[128,1280]{1,0:T(8,128)(2,1)S(1)} %expert.2), channel_id=1, source_target_pairs={{0,128},{16,144},{128,0},{144,16},{1,129},{17,145},{129,1},{145,17... | collective-permute-start | bytes 983048 | tf_op jit(solution)/shard_map/ppermute | solution.py:254
  60.3 4.1 %collective-permute-done.4.other_a_ref = bf16[128,1280]{1,0:T(8,128)(2,1)S(1)} collective-permute-done((bf16[128,1280]{1,0:T(8,128)(2,1)S(1)}, bf16[128,1280]{1,0:T(8,128)(2,1)S(1)}, u32[]{:S(2)}, u32[]{:S(2)}) %collective-permute-start.4) | collective-permute-done | bytes 327712 | tf_op jit(solution)/shard_map/ppermute | solution.py:254
  64.4 0.0 collective-permute-done.5.other_b_ref
  64.4 7.0 %collective-permute-done.1.own_b_ref = bf16[128,1280]{1,0:T(8,128)(2,1)S(1)} collective-permute-done((bf16[128,1280]{1,0:T(8,128)(2,1)S(1)}, bf16[128,1280]{1,0:T(8,128)(2,1)S(1)}, u32[]{:S(2)}, u32[]{:S(2)}) %collective-permute-start.1) | collective-permute-done | bytes 327712 | tf_op jit(solution)/shard_map/ppermute | solution.py:254
  71.4 0.2 add_parts.1
  71.7 26.8 %all_to_all.11.slots_ref = bf16[64,2,2,1280]{3,2,1,0:T(2,128)(2,1)S(1)} all-to-all(bf16[64,2,2,1280]{3,2,1,0:T(2,128)(2,1)S(1)} %add_parts.1), channel_id=1, replica_groups=mesh['dp'=2,'x'=4,'y_lo'=2,'z'=8,'core'=2] {'x','z','core'}, dimensions={0} | all-to-all | bytes 1310720 | tf_op jit(solution)/shard_map/all_to_all | solution.py:258
  98.5 0.0 copy-done.2
  98.5 1.4 %mix.1 = bf16[2,256,1280]{2,1,0:T(8,128)(2,1)} custom-call(bf16[2,256,256]{2,1,0:T(8,128)(2,1)S(1)} %copy-done.2, bf16[64,2,2,1280]{3,2,1,0:T(2,128)(2,1)S(1)} %all_to_all.11.slots_ref), custom_call_target="tpu_custom_call" | custom-call | tf_op jit(solution)/shard_map/mix/pallas_call | solution.py:242
Async XLA Ops:
  0.0 42.9 %copy-start = (bf16[1,1280,1280]{2,1,0:T(8,128)(2,1)S(1)}, bf16[1,1280,1280]{2,1,0:T(8,128)(2,1)}, u32[]{:S(2)}) copy-start(bf16[1,1280,1280]{2,1,0:T(8,128)(2,1)} %up_hbm.1) | copy-start | bytes 9830404
  38.8 10.5 %collective-permute-start.3 = (bf16[128,1280]{1,0:T(8,128)(2,1)S(1)}, bf16[128,1280]{1,0:T(8,128)(2,1)S(1)}, u32[]{:S(2)}, u32[]{:S(2)}) collective-permute-start(bf16[128,1280]{1,0:T(8,128)(2,1)S(1)} %get-tuple-element.20), channel_id=1, source_target_pairs={{16,128},{144,0},{128,16},{0,144},{17,129},{145,1},{129,17},{1,145... | collective-permute-start | bytes 983048 | tf_op jit(solution)/shard_map/ppermute | solution.py:254
  41.6 8.7 %collective-permute-start.2 = (bf16[128,1280]{1,0:T(8,128)(2,1)S(1)}, bf16[128,1280]{1,0:T(8,128)(2,1)S(1)}, u32[]{:S(2)}, u32[]{:S(2)}) collective-permute-start(bf16[128,1280]{1,0:T(8,128)(2,1)S(1)} %get-tuple-element.20), channel_id=1, source_target_pairs={{0,16},{128,144},{16,0},{144,128},{1,17},{129,145},{17,1},{145,129... | collective-permute-start | bytes 983048 | tf_op jit(solution)/shard_map/ppermute | solution.py:254
  41.6 15.7 %collective-permute-start = (bf16[128,1280]{1,0:T(8,128)(2,1)S(1)}, bf16[128,1280]{1,0:T(8,128)(2,1)S(1)}, u32[]{:S(2)}, u32[]{:S(2)}) collective-permute-start(bf16[128,1280]{1,0:T(8,128)(2,1)S(1)} %get-tuple-element.16.rows_ref), channel_id=1, source_target_pairs={{0,128},{16,144},{128,0},{144,16},{1,129},{17,145},{129,1},{145,17... | collective-permute-start | bytes 983048 | tf_op jit(solution)/shard_map/ppermute | solution.py:254
  42.9 1.9 %copy-start.1 = (bf16[1,1280,1280]{2,1,0:T(8,128)(2,1)S(1)}, bf16[1,1280,1280]{2,1,0:T(8,128)(2,1)}, u32[]{:S(2)}) copy-start(bf16[1,1280,1280]{2,1,0:T(8,128)(2,1)} %down_hbm.1) | copy-start | bytes 9830404
  52.3 12.1 %collective-permute-start.4 = (bf16[128,1280]{1,0:T(8,128)(2,1)S(1)}, bf16[128,1280]{1,0:T(8,128)(2,1)S(1)}, u32[]{:S(2)}, u32[]{:S(2)}) collective-permute-start(bf16[128,1280]{1,0:T(8,128)(2,1)S(1)} %get-tuple-element.21), channel_id=1, source_target_pairs={{0,16},{128,144},{16,0},{144,128},{1,17},{129,145},{17,1},{145,129... | collective-permute-start | bytes 983048 | tf_op jit(solution)/shard_map/ppermute | solution.py:254
  52.6 11.8 %collective-permute-start.5 = (bf16[128,1280]{1,0:T(8,128)(2,1)S(1)}, bf16[128,1280]{1,0:T(8,128)(2,1)S(1)}, u32[]{:S(2)}, u32[]{:S(2)}) collective-permute-start(bf16[128,1280]{1,0:T(8,128)(2,1)S(1)} %get-tuple-element.22), channel_id=1, source_target_pairs={{16,128},{144,0},{128,16},{0,144},{17,129},{145,1},{129,17},{1,145... | collective-permute-start | bytes 983048 | tf_op jit(solution)/shard_map/ppermute | solution.py:254
  58.5 39.9 %copy-start.2 = (bf16[2,256,256]{2,1,0:T(8,128)(2,1)S(1)}, bf16[2,256,256]{2,1,0:T(8,128)(2,1)}, u32[]{:S(2)}) copy-start(bf16[2,256,256]{2,1,0:T(8,128)(2,1)} %get-tuple-element.14.combine_ref) | copy-start | bytes 786436
  58.5 12.9 %collective-permute-start.1 = (bf16[128,1280]{1,0:T(8,128)(2,1)S(1)}, bf16[128,1280]{1,0:T(8,128)(2,1)S(1)}, u32[]{:S(2)}, u32[]{:S(2)}) collective-permute-start(bf16[128,1280]{1,0:T(8,128)(2,1)S(1)} %expert.2), channel_id=1, source_target_pairs={{0,128},{16,144},{128,0},{144,16},{1,129},{17,145},{129,1},{145,17... | collective-permute-start | bytes 983048 | tf_op jit(solution)/shard_map/ppermute | solution.py:254

commit v5 on v4

--- a/solution.py
+++ b/solution.py
@@ -14,7 +14,7 @@
 INNER = 16
 PLANE = ("x", "z", "core")
 RING = ("dp", "y_lo")
-EVEN, ODD, ACROSS = ((0, 1), (2, 3)), ((1, 2), (3, 0)), ((0, 2), (1, 3))
+FIRST, SECOND, ACROSS = ((3, 2, 1, 0), (1, 0, 3, 2)), ((1, 0, 3, 2), (3, 2, 1, 0)), ((2, 3, 0, 1), (2, 3, 0, 1))
 IMAGES = 2
 VMEM = pl.BlockSpec(memory_space=pltpu.VMEM)
 HBM = pl.BlockSpec(memory_space=pltpu.HBM)
@@ -199,23 +199,38 @@
     )(arrived)
 
 
-def add_kernel(own_a_ref, own_b_ref, other_a_ref, other_b_ref, out_ref):
+def add_kernel(a_ref, b_ref, out_ref):
+    out_ref[...] = (a_ref[...].astype(F32) + b_ref[...].astype(F32)).astype(BF16)
+
+
+def add(a, b):
+    return pl.pallas_call(
+        add_kernel,
+        in_specs=[VMEM] * 2,
+        out_specs=VMEM,
+        out_shape=jax.ShapeDtypeStruct(a.shape, BF16),
+        compiler_params=limit(16),
+        name="add",
+    )(a, b)
+
+
+def join_kernel(own_ref, a_ref, b_ref, out_ref):
     places, _, images, width = out_ref.shape
-    for group, (a_ref, b_ref) in enumerate([(own_a_ref, own_b_ref), (other_a_ref, other_b_ref)]):
-        total = (a_ref[...].astype(F32) + b_ref[...].astype(F32)).astype(BF16)
-        out_ref[:, group, :, :] = total.reshape(places, images, width)
-
-
-def add_parts(own, other):
-    rows, width = own[0].shape
-    return pl.pallas_call(
-        add_kernel,
-        in_specs=[VMEM] * 4,
+    out_ref[:, 0, :, :] = own_ref[...].reshape(places, images, width)
+    total = (a_ref[...].astype(F32) + b_ref[...].astype(F32)).astype(BF16)
+    out_ref[:, 1, :, :] = total.reshape(places, images, width)
+
+
+def join(own, a, b):
+    rows, width = own.shape
+    return pl.pallas_call(
+        join_kernel,
+        in_specs=[VMEM] * 3,
         out_specs=VMEM,
         out_shape=jax.ShapeDtypeStruct((rows // IMAGES, 2, IMAGES, width), BF16),
         compiler_params=limit(16),
-        name="add_parts",
-    )(*own, *other)
+        name="join",
+    )(own, a, b)
 
 
 def mix_kernel(combine_ref, slots_ref, out_hbm, out_ref, sems):
@@ -250,8 +265,9 @@
     )(combine, slot_outputs)
 
 
-def pairwise(value, pairs):
-    return lax.ppermute(value, RING, [(a, b) for a, b in pairs] + [(b, a) for a, b in pairs])
+def send(value, targets, back=False):
+    pairs = [(2 * at + core, 2 * to + core) for core in range(2) for at, to in enumerate(targets[core])]
+    return lax.ppermute(value, RING + ("core",), [pair[::-1] if back else pair for pair in pairs])
 
 
 def exchange(value):
@@ -260,15 +276,18 @@
 
 def local(tokens, norm_gain, slot_params, logit_scale, expert_up, expert_down):
     slot_inputs, combine = route(tokens, norm_gain, slot_params, logit_scale)
-    arrived = exchange(slot_inputs)
-    own, other = split(arrived)
-    odd, even = pairwise(other, ODD), pairwise(other, EVEN)
-    across = pairwise(own, ACROSS)
+    own, other = split(exchange(slot_inputs))
+    across, first, second = send(own, ACROSS), send(other, FIRST), send(other, SECOND)
     kept, up_matrix, down_matrix = first_expert(own, expert_up, expert_down)
-    even, odd = expert([even, odd], up_matrix, down_matrix)
-    odd, even = pairwise(odd, ODD), pairwise(even, EVEN)
     (across,) = expert([across], up_matrix, down_matrix)
-    slot_outputs = add_parts((kept, pairwise(across, ACROSS)), (even, odd))
+    first, _ = lax.optimization_barrier((first, across))
+    across = send(across, ACROSS, True)
+    (first,) = expert([first], up_matrix, down_matrix)
+    second, _ = lax.optimization_barrier((second, first))
+    first = send(first, FIRST, True)
+    (second,) = expert([second], up_matrix, down_matrix)
+    second = send(second, SECOND, True)
+    slot_outputs = join(add(kept, across), first, second)
     return mix(combine, exchange(slot_outputs))
 
 

time: 100 us -> 99.3 us (level)
  waiting for transfers between devices: 17.5 us -> 15.4 us
  starting transfers between devices: 7.58 us -> 9.25 us
    ppermute x6, waiting for transfers between devices: 17.5 us -> 15.4 us  [send(): lax.ppermute(value, RING + ('core',), [pair[::-1] if back else pair for p...]
    ppermute x6, starting transfers between devices: 7.58 us -> 9.25 us  [send(): lax.ppermute(value, RING + ('core',), [pair[::-1] if back else pair for p...]
    pallas_call x2 -> x3, Pallas kernels: 3.16 us -> 3.47 us  [expert(): pl.pallas_call(lambda *refs: expert_kernel(len(groups), *refs), in_specs=...]
where the time goes in v5:
time: 99.3 us; the launch traced here: 99.1 us
  blocking collectives  59.2 us (60%)
  waiting for transfers between devices  15.4 us (16%)
  Pallas kernels  12.4 us (12%)
  starting transfers between devices  9.25 us (9%)
  local copies, waits for them, and re-layouts  1.93 us (2%)
    all_to_all x2, blocking collectives, exchange(): return lax.all_to_all(value, PLANE, split_axis=0, concat_axis=0, tiled=True)  59.2 us
    ppermute x6, waiting for transfers between devices, send(): lax.ppermute(value, RING + ('core',), [pair[::-1] if back else pair for p...  15.4 us
    ppermute x6, starting transfers between devices, send(): lax.ppermute(value, RING + ('core',), [pair[::-1] if back else pair for p...  9.25 us
    pallas_call x1, Pallas kernels, route(): pl.pallas_call(route_kernel, in_specs=[HBM] * 4, out_specs=[HBM] * 2, out...  4.78 us
    pallas_call x3, Pallas kernels, expert(): pl.pallas_call(lambda *refs: expert_kernel(len(groups), *refs), in_specs=...  3.47 us
    pallas_call x1, Pallas kernels, first_expert(): pl.pallas_call(first_expert_kernel, in_specs=[VMEM, HBM, HBM], out_specs=...  2.39 us
  transfers between devices with their start and end apart: 6, of which 5 were waited for; matrix products, arithmetic and copies ran while one was open for 0% of the time, Pallas kernels for 6%

profile of v5, /device:TPU:1, one launch (start us, length us, event | category | flops | bytes accessed | tf_op | source)
XLA Modules:
  0.0 99.1 jit_solution(6773341114726552800)
XLA Ops:
  0.0 0.0 copy-start
  0.8 4.8 %route.1 = (bf16[64,2,2,1280]{3,2,1,0:T(2,128)(2,1)}, bf16[2,256,256]{2,1,0:T(8,128)(2,1)}) custom-call(bf16[2,256,1280]{2,1,0:T(8,128)(2,1)} %tokens_hbm.1, f32[1280]{0:T(1024)} %gain_hbm.1, bf16[1280,128]{1,0:T(8,128)(2,1)} %params_hbm.1, f32[1]{0:T(128)S(6)} %copy.7.scale_hbm), custom_call_target="tpu_custom_call" | custom-call | tf_op jit(solution)/shard_map/route/pallas_call | solution.py:105
  5.6 33.1 %all_to_all.10.arrived_ref = bf16[64,2,2,1280]{3,2,1,0:T(2,128)(2,1)S(1)} all-to-all(bf16[64,2,2,1280]{3,2,1,0:T(2,128)(2,1)} %get-tuple-element.15), channel_id=1, replica_groups=mesh['dp'=2,'x'=4,'y_lo'=2,'z'=8,'core'=2] {'x','z','core'}, dimensions={0} | all-to-all | bytes 1310720 | tf_op jit(solution)/shard_map/all_to_all | solution.py:274
  38.7 0.1 split.1
  38.8 3.0 %collective-permute-start = (bf16[128,1280]{1,0:T(8,128)(2,1)S(1)}, bf16[128,1280]{1,0:T(8,128)(2,1)S(1)}, u32[]{:S(2)}, u32[]{:S(2)}) collective-permute-start(bf16[128,1280]{1,0:T(8,128)(2,1)S(1)} %get-tuple-element.16.rows_ref), channel_id=1, source_target_pairs={{0,128},{16,144},{128,0},{144,16},{1,129},{17,145},{129,1},{145,17... | collective-permute-start | bytes 983048 | tf_op jit(solution)/shard_map/ppermute | solution.py:270
  41.8 0.4 collective-permute-start.2
  42.2 0.4 collective-permute-start.4
  42.6 0.0 copy-done
  42.6 0.0 copy-start.1
  42.6 1.9 %copy-done.1 = bf16[1,1280,1280]{2,1,0:T(8,128)(2,1)S(1)} copy-done((bf16[1,1280,1280]{2,1,0:T(8,128)(2,1)S(1)}, bf16[1,1280,1280]{2,1,0:T(8,128)(2,1)}, u32[]{:S(2)}) %copy-start.1) | copy-done | bytes 3276824
  44.5 2.4 %first_expert.1 = (bf16[128,1280]{1,0:T(8,128)(2,1)S(1)}, bf16[1280,1280]{1,0:T(8,128)(2,1)S(1)}, bf16[1280,1280]{1,0:T(8,128)(2,1)S(1)}) custom-call(bf16[128,1280]{1,0:T(8,128)(2,1)S(1)} %get-tuple-element.16.rows_ref, bf16[1,1280,1280]{2,1,0:T(8,128)(2,1)S(1)} %copy-done, bf16[1,1280,1280]{2,1,0:T(8,128)(2,1)S(1)} %copy-done.1), custom_call_target="tpu_custom_call" | custom-call | tf_op jit(solution)/shard_map/first_expert/pallas_call | solution.py:147
  46.9 2.5 %collective-permute-done.refs_0_ = bf16[128,1280]{1,0:T(8,128)(2,1)S(1)} collective-permute-done((bf16[128,1280]{1,0:T(8,128)(2,1)S(1)}, bf16[128,1280]{1,0:T(8,128)(2,1)S(1)}, u32[]{:S(2)}, u32[]{:S(2)}) %collective-permute-start) | collective-permute-done | bytes 327712 | tf_op jit(solution)/shard_map/ppermute | solution.py:270
  49.5 1.2 %expert.3 = bf16[128,1280]{1,0:T(8,128)(2,1)S(1)} custom-call(bf16[128,1280]{1,0:T(8,128)(2,1)S(1)} %collective-permute-done.refs_0_, bf16[1280,1280]{1,0:T(8,128)(2,1)S(1)} %get-tuple-element.18.refs_1_, bf16[1280,1280]{1,0:T(8,128)(2,1)S(1)} %get-tuple-element.19.refs_2_), custom_call_target="tpu_custom_call" | custom-call | tf_op jit(solution)/shard_map/expert/pallas_call | solution.py:174
  50.6 3.0 %collective-permute-start.1 = (bf16[128,1280]{1,0:T(8,128)(2,1)S(1)}, bf16[128,1280]{1,0:T(8,128)(2,1)S(1)}, u32[]{:S(2)}, u32[]{:S(2)}) collective-permute-start(bf16[128,1280]{1,0:T(8,128)(2,1)S(1)} %expert.3), channel_id=1, source_target_pairs={{128,0},{144,16},{0,128},{16,144},{129,1},{145,17},{1,129},{17,145... | collective-permute-start | bytes 983048 | tf_op jit(solution)/shard_map/ppermute | solution.py:270
  53.6 3.2 %collective-permute-done.2.refs_0_ = bf16[128,1280]{1,0:T(8,128)(2,1)S(1)} collective-permute-done((bf16[128,1280]{1,0:T(8,128)(2,1)S(1)}, bf16[128,1280]{1,0:T(8,128)(2,1)S(1)}, u32[]{:S(2)}, u32[]{:S(2)}) %collective-permute-start.2) | collective-permute-done | bytes 327712 | tf_op jit(solution)/shard_map/ppermute | solution.py:270
  56.8 1.2 %expert.4 = bf16[128,1280]{1,0:T(8,128)(2,1)S(1)} custom-call(bf16[128,1280]{1,0:T(8,128)(2,1)S(1)} %collective-permute-done.2.refs_0_, bf16[1280,1280]{1,0:T(8,128)(2,1)S(1)} %get-tuple-element.18.refs_1_, bf16[1280,1280]{1,0:T(8,128)(2,1)S(1)} %get-tuple-element.19.refs_2_), custom_call_target="tpu_custom_call" | custom-call | tf_op jit(solution)/shard_map/expert/pallas_call | solution.py:174
  58.0 0.0 collective-permute-done.4.refs_0_
  58.0 1.2 %expert.5 = bf16[128,1280]{1,0:T(8,128)(2,1)S(1)} custom-call(bf16[128,1280]{1,0:T(8,128)(2,1)S(1)} %collective-permute-done.4.refs_0_, bf16[1280,1280]{1,0:T(8,128)(2,1)S(1)} %get-tuple-element.18.refs_1_, bf16[1280,1280]{1,0:T(8,128)(2,1)S(1)} %get-tuple-element.19.refs_2_), custom_call_target="tpu_custom_call" | custom-call | tf_op jit(solution)/shard_map/expert/pallas_call | solution.py:174
  59.2 0.0 copy-start.2
  59.2 2.5 %collective-permute-start.5 = (bf16[128,1280]{1,0:T(8,128)(2,1)S(1)}, bf16[128,1280]{1,0:T(8,128)(2,1)S(1)}, u32[]{:S(2)}, u32[]{:S(2)}) collective-permute-start(bf16[128,1280]{1,0:T(8,128)(2,1)S(1)} %expert.5), channel_id=1, source_target_pairs={{16,0},{0,16},{144,128},{128,144},{145,1},{129,17},{17,129},{1,145... | collective-permute-start | bytes 983048 | tf_op jit(solution)/shard_map/ppermute | solution.py:270
  61.6 0.0 collective-permute-start.3
  61.6 1.9 %collective-permute-done.1.b_ref = bf16[128,1280]{1,0:T(8,128)(2,1)S(1)} collective-permute-done((bf16[128,1280]{1,0:T(8,128)(2,1)S(1)}, bf16[128,1280]{1,0:T(8,128)(2,1)S(1)}, u32[]{:S(2)}, u32[]{:S(2)}) %collective-permute-start.1) | collective-permute-done | bytes 327712 | tf_op jit(solution)/shard_map/ppermute | solution.py:270
  63.5 0.1 add.1.own_ref
  63.6 5.7 %collective-permute-done.5.b_ref = bf16[128,1280]{1,0:T(8,128)(2,1)S(1)} collective-permute-done((bf16[128,1280]{1,0:T(8,128)(2,1)S(1)}, bf16[128,1280]{1,0:T(8,128)(2,1)S(1)}, u32[]{:S(2)}, u32[]{:S(2)}) %collective-permute-start.5) | collective-permute-done | bytes 327712 | tf_op jit(solution)/shard_map/ppermute | solution.py:270
  69.3 2.2 %collective-permute-done.3.a_ref = bf16[128,1280]{1,0:T(8,128)(2,1)S(1)} collective-permute-done((bf16[128,1280]{1,0:T(8,128)(2,1)S(1)}, bf16[128,1280]{1,0:T(8,128)(2,1)S(1)}, u32[]{:S(2)}, u32[]{:S(2)}) %collective-permute-start.3) | collective-permute-done | bytes 327712 | tf_op jit(solution)/shard_map/ppermute | solution.py:270
  71.4 0.2 join.1
  71.6 26.1 %all_to_all.11.slots_ref = bf16[64,2,2,1280]{3,2,1,0:T(2,128)(2,1)S(1)} all-to-all(bf16[64,2,2,1280]{3,2,1,0:T(2,128)(2,1)S(1)} %join.1), channel_id=1, replica_groups=mesh['dp'=2,'x'=4,'y_lo'=2,'z'=8,'core'=2] {'x','z','core'}, dimensions={0} | all-to-all | bytes 1310720 | tf_op jit(solution)/shard_map/all_to_all | solution.py:274
  97.7 0.0 copy-done.2
  97.7 1.4 %mix.1 = bf16[2,256,1280]{2,1,0:T(8,128)(2,1)} custom-call(bf16[2,256,256]{2,1,0:T(8,128)(2,1)S(1)} %copy-done.2, bf16[64,2,2,1280]{3,2,1,0:T(2,128)(2,1)S(1)} %all_to_all.11.slots_ref), custom_call_target="tpu_custom_call" | custom-call | tf_op jit(solution)/shard_map/mix/pallas_call | solution.py:257
Async XLA Ops:
  0.0 42.6 %copy-start = (bf16[1,1280,1280]{2,1,0:T(8,128)(2,1)S(1)}, bf16[1,1280,1280]{2,1,0:T(8,128)(2,1)}, u32[]{:S(2)}) copy-start(bf16[1,1280,1280]{2,1,0:T(8,128)(2,1)} %up_hbm.1) | copy-start | bytes 9830404
  38.8 10.6 %collective-permute-start = (bf16[128,1280]{1,0:T(8,128)(2,1)S(1)}, bf16[128,1280]{1,0:T(8,128)(2,1)S(1)}, u32[]{:S(2)}, u32[]{:S(2)}) collective-permute-start(bf16[128,1280]{1,0:T(8,128)(2,1)S(1)} %get-tuple-element.16.rows_ref), channel_id=1, source_target_pairs={{0,128},{16,144},{128,0},{144,16},{1,129},{17,145},{129,1},{145,17... | collective-permute-start | bytes 983048 | tf_op jit(solution)/shard_map/ppermute | solution.py:270
  41.8 15.0 %collective-permute-start.2 = (bf16[128,1280]{1,0:T(8,128)(2,1)S(1)}, bf16[128,1280]{1,0:T(8,128)(2,1)S(1)}, u32[]{:S(2)}, u32[]{:S(2)}) collective-permute-start(bf16[128,1280]{1,0:T(8,128)(2,1)S(1)} %get-tuple-element.20), channel_id=1, source_target_pairs={{0,144},{16,128},{128,16},{144,0},{1,17},{17,1},{129,145},{145,129... | collective-permute-start | bytes 983048 | tf_op jit(solution)/shard_map/ppermute | solution.py:270
  42.2 15.8 %collective-permute-start.4 = (bf16[128,1280]{1,0:T(8,128)(2,1)S(1)}, bf16[128,1280]{1,0:T(8,128)(2,1)S(1)}, u32[]{:S(2)}, u32[]{:S(2)}) collective-permute-start(bf16[128,1280]{1,0:T(8,128)(2,1)S(1)} %get-tuple-element.20), channel_id=1, source_target_pairs={{0,16},{16,0},{128,144},{144,128},{1,145},{17,129},{129,17},{145,1... | collective-permute-start | bytes 983048 | tf_op jit(solution)/shard_map/ppermute | solution.py:270
  42.6 1.9 %copy-start.1 = (bf16[1,1280,1280]{2,1,0:T(8,128)(2,1)S(1)}, bf16[1,1280,1280]{2,1,0:T(8,128)(2,1)}, u32[]{:S(2)}) copy-start(bf16[1,1280,1280]{2,1,0:T(8,128)(2,1)} %down_hbm.1) | copy-start | bytes 9830404
  50.6 12.9 %collective-permute-start.1 = (bf16[128,1280]{1,0:T(8,128)(2,1)S(1)}, bf16[128,1280]{1,0:T(8,128)(2,1)S(1)}, u32[]{:S(2)}, u32[]{:S(2)}) collective-permute-start(bf16[128,1280]{1,0:T(8,128)(2,1)S(1)} %expert.3), channel_id=1, source_target_pairs={{128,0},{144,16},{0,128},{16,144},{129,1},{145,17},{1,129},{17,145... | collective-permute-start | bytes 983048 | tf_op jit(solution)/shard_map/ppermute | solution.py:270
  59.2 38.6 %copy-start.2 = (bf16[2,256,256]{2,1,0:T(8,128)(2,1)S(1)}, bf16[2,256,256]{2,1,0:T(8,128)(2,1)}, u32[]{:S(2)}) copy-start(bf16[2,256,256]{2,1,0:T(8,128)(2,1)} %get-tuple-element.14.combine_ref) | copy-start | bytes 786436
  59.2 10.1 %collective-permute-start.5 = (bf16[128,1280]{1,0:T(8,128)(2,1)S(1)}, bf16[128,1280]{1,0:T(8,128)(2,1)S(1)}, u32[]{:S(2)}, u32[]{:S(2)}) collective-permute-start(bf16[128,1280]{1,0:T(8,128)(2,1)S(1)} %expert.5), channel_id=1, source_target_pairs={{16,0},{0,16},{144,128},{128,144},{145,1},{129,17},{17,129},{1,145... | collective-permute-start | bytes 983048 | tf_op jit(solution)/shard_map/ppermute | solution.py:270
  61.6 9.8 %collective-permute-start.3 = (bf16[128,1280]{1,0:T(8,128)(2,1)S(1)}, bf16[128,1280]{1,0:T(8,128)(2,1)S(1)}, u32[]{:S(2)}, u32[]{:S(2)}) collective-permute-start(bf16[128,1280]{1,0:T(8,128)(2,1)S(1)} %expert.4), channel_id=1, source_target_pairs={{144,0},{128,16},{16,128},{0,144},{17,1},{1,17},{145,129},{129,145... | collective-permute-start | bytes 983048 | tf_op jit(solution)/shard_map/ppermute | solution.py:270

commit v6 on v5

--- a/solution.py
+++ b/solution.py
@@ -14,7 +14,7 @@
 INNER = 16
 PLANE = ("x", "z", "core")
 RING = ("dp", "y_lo")
-FIRST, SECOND, ACROSS = ((3, 2, 1, 0), (1, 0, 3, 2)), ((1, 0, 3, 2), (3, 2, 1, 0)), ((2, 3, 0, 1), (2, 3, 0, 1))
+FIRST, SECOND, ACROSS = ((1, 2, 3, 0), (1, 2, 3, 0)), ((3, 0, 1, 2), (3, 0, 1, 2)), ((2, 3, 0, 1), (2, 3, 0, 1))
 IMAGES = 2
 VMEM = pl.BlockSpec(memory_space=pltpu.VMEM)
 HBM = pl.BlockSpec(memory_space=pltpu.HBM)

time: 99.3 us -> 99.3 us (level)
  waiting for transfers between devices: 15.4 us -> 12.3 us
  starting transfers between devices: 9.25 us -> 11.4 us
  blocking collectives: 59.2 us -> 60.2 us
    ppermute x6, waiting for transfers between devices: 15.4 us -> 12.3 us  [send(): lax.ppermute(value, RING + ('core',), [pair[::-1] if back else pair for p...]
    ppermute x6, starting transfers between devices: 9.25 us -> 11.4 us  [send(): lax.ppermute(value, RING + ('core',), [pair[::-1] if back else pair for p...]
where the time goes in v6:
time: 99.3 us; the launch traced here: 99.1 us
  blocking collectives  60.2 us (61%)
  Pallas kernels  12.4 us (12%)
  waiting for transfers between devices  12.3 us (12%)
  starting transfers between devices  11.4 us (11%)
  local copies, waits for them, and re-layouts  1.93 us (2%)
    all_to_all x2, blocking collectives, exchange(): return lax.all_to_all(value, PLANE, split_axis=0, concat_axis=0, tiled=True)  60.2 us
    ppermute x6, waiting for transfers between devices, send(): lax.ppermute(value, RING + ('core',), [pair[::-1] if back else pair for p...  12.3 us
    ppermute x6, starting transfers between devices, send(): lax.ppermute(value, RING + ('core',), [pair[::-1] if back else pair for p...  11.4 us
    pallas_call x1, Pallas kernels, route(): pl.pallas_call(route_kernel, in_specs=[HBM] * 4, out_specs=[HBM] * 2, out...  4.78 us
    pallas_call x3, Pallas kernels, expert(): pl.pallas_call(lambda *refs: expert_kernel(len(groups), *refs), in_specs=...  3.47 us
    pallas_call x1, Pallas kernels, first_expert(): pl.pallas_call(first_expert_kernel, in_specs=[VMEM, HBM, HBM], out_specs=...  2.39 us
  transfers between devices with their start and end apart: 6, of which 5 were waited for; matrix products, arithmetic and copies ran while one was open for 0% of the time, Pallas kernels for 6%

profile of v6, /device:TPU:1, one launch (start us, length us, event | category | flops | bytes accessed | tf_op | source)
XLA Modules:
  0.0 99.1 jit_solution(1518714962537794365)
XLA Ops:
  0.0 0.0 copy-start
  0.8 4.8 %route.1 = (bf16[64,2,2,1280]{3,2,1,0:T(2,128)(2,1)}, bf16[2,256,256]{2,1,0:T(8,128)(2,1)}) custom-call(bf16[2,256,1280]{2,1,0:T(8,128)(2,1)} %tokens_hbm.1, f32[1280]{0:T(1024)} %gain_hbm.1, bf16[1280,128]{1,0:T(8,128)(2,1)} %params_hbm.1, f32[1]{0:T(128)S(6)} %copy.7.scale_hbm), custom_call_target="tpu_custom_call" | custom-call | tf_op jit(solution)/shard_map/route/pallas_call | solution.py:105
  5.6 33.1 %all_to_all.10.arrived_ref = bf16[64,2,2,1280]{3,2,1,0:T(2,128)(2,1)S(1)} all-to-all(bf16[64,2,2,1280]{3,2,1,0:T(2,128)(2,1)} %get-tuple-element.15), channel_id=1, replica_groups=mesh['dp'=2,'x'=4,'y_lo'=2,'z'=8,'core'=2] {'x','z','core'}, dimensions={0} | all-to-all | bytes 1310720 | tf_op jit(solution)/shard_map/all_to_all | solution.py:274
  38.7 0.1 split.1
  38.8 3.0 %collective-permute-start = (bf16[128,1280]{1,0:T(8,128)(2,1)S(1)}, bf16[128,1280]{1,0:T(8,128)(2,1)S(1)}, u32[]{:S(2)}, u32[]{:S(2)}) collective-permute-start(bf16[128,1280]{1,0:T(8,128)(2,1)S(1)} %get-tuple-element.16.rows_ref), channel_id=1, source_target_pairs={{0,128},{16,144},{128,0},{144,16},{1,129},{17,145},{129,1},{145,17... | collective-permute-start | bytes 983048 | tf_op jit(solution)/shard_map/ppermute | solution.py:270
  41.8 0.4 collective-permute-start.2
  42.2 2.3 %collective-permute-start.4 = (bf16[128,1280]{1,0:T(8,128)(2,1)S(1)}, bf16[128,1280]{1,0:T(8,128)(2,1)S(1)}, u32[]{:S(2)}, u32[]{:S(2)}) collective-permute-start(bf16[128,1280]{1,0:T(8,128)(2,1)S(1)} %get-tuple-element.20), channel_id=1, source_target_pairs={{0,144},{16,0},{128,16},{144,128},{1,145},{17,1},{129,17},{145,129... | collective-permute-start | bytes 983048 | tf_op jit(solution)/shard_map/ppermute | solution.py:270
  44.5 0.0 copy-done
  44.5 0.0 copy-start.1
  44.5 1.9 %copy-done.1 = bf16[1,1280,1280]{2,1,0:T(8,128)(2,1)S(1)} copy-done((bf16[1,1280,1280]{2,1,0:T(8,128)(2,1)S(1)}, bf16[1,1280,1280]{2,1,0:T(8,128)(2,1)}, u32[]{:S(2)}) %copy-start.1) | copy-done | bytes 3276824
  46.4 2.4 %first_expert.1 = (bf16[128,1280]{1,0:T(8,128)(2,1)S(1)}, bf16[1280,1280]{1,0:T(8,128)(2,1)S(1)}, bf16[1280,1280]{1,0:T(8,128)(2,1)S(1)}) custom-call(bf16[128,1280]{1,0:T(8,128)(2,1)S(1)} %get-tuple-element.16.rows_ref, bf16[1,1280,1280]{2,1,0:T(8,128)(2,1)S(1)} %copy-done, bf16[1,1280,1280]{2,1,0:T(8,128)(2,1)S(1)} %copy-done.1), custom_call_target="tpu_custom_call" | custom-call | tf_op jit(solution)/shard_map/first_expert/pallas_call | solution.py:147
  48.8 0.6 collective-permute-done.refs_0_
  49.5 1.2 %expert.3 = bf16[128,1280]{1,0:T(8,128)(2,1)S(1)} custom-call(bf16[128,1280]{1,0:T(8,128)(2,1)S(1)} %collective-permute-done.refs_0_, bf16[1280,1280]{1,0:T(8,128)(2,1)S(1)} %get-tuple-element.18.refs_1_, bf16[1280,1280]{1,0:T(8,128)(2,1)S(1)} %get-tuple-element.19.refs_2_), custom_call_target="tpu_custom_call" | custom-call | tf_op jit(solution)/shard_map/expert/pallas_call | solution.py:174
  50.6 3.0 %collective-permute-start.1 = (bf16[128,1280]{1,0:T(8,128)(2,1)S(1)}, bf16[128,1280]{1,0:T(8,128)(2,1)S(1)}, u32[]{:S(2)}, u32[]{:S(2)}) collective-permute-start(bf16[128,1280]{1,0:T(8,128)(2,1)S(1)} %expert.3), channel_id=1, source_target_pairs={{128,0},{144,16},{0,128},{16,144},{129,1},{145,17},{1,129},{17,145... | collective-permute-start | bytes 983048 | tf_op jit(solution)/shard_map/ppermute | solution.py:270
  53.6 4.0 %collective-permute-done.2.refs_0_ = bf16[128,1280]{1,0:T(8,128)(2,1)S(1)} collective-permute-done((bf16[128,1280]{1,0:T(8,128)(2,1)S(1)}, bf16[128,1280]{1,0:T(8,128)(2,1)S(1)}, u32[]{:S(2)}, u32[]{:S(2)}) %collective-permute-start.2) | collective-permute-done | bytes 327712 | tf_op jit(solution)/shard_map/ppermute | solution.py:270
  57.6 1.2 %expert.4 = bf16[128,1280]{1,0:T(8,128)(2,1)S(1)} custom-call(bf16[128,1280]{1,0:T(8,128)(2,1)S(1)} %collective-permute-done.2.refs_0_, bf16[1280,1280]{1,0:T(8,128)(2,1)S(1)} %get-tuple-element.18.refs_1_, bf16[1280,1280]{1,0:T(8,128)(2,1)S(1)} %get-tuple-element.19.refs_2_), custom_call_target="tpu_custom_call" | custom-call | tf_op jit(solution)/shard_map/expert/pallas_call | solution.py:174
  58.8 0.0 collective-permute-done.4.refs_0_
  58.8 1.2 %expert.5 = bf16[128,1280]{1,0:T(8,128)(2,1)S(1)} custom-call(bf16[128,1280]{1,0:T(8,128)(2,1)S(1)} %collective-permute-done.4.refs_0_, bf16[1280,1280]{1,0:T(8,128)(2,1)S(1)} %get-tuple-element.18.refs_1_, bf16[1280,1280]{1,0:T(8,128)(2,1)S(1)} %get-tuple-element.19.refs_2_), custom_call_target="tpu_custom_call" | custom-call | tf_op jit(solution)/shard_map/expert/pallas_call | solution.py:174
  60.0 0.0 copy-start.2
  60.0 0.3 collective-permute-start.5
  60.3 2.4 %collective-permute-start.3 = (bf16[128,1280]{1,0:T(8,128)(2,1)S(1)}, bf16[128,1280]{1,0:T(8,128)(2,1)S(1)}, u32[]{:S(2)}, u32[]{:S(2)}) collective-permute-start(bf16[128,1280]{1,0:T(8,128)(2,1)S(1)} %expert.4), channel_id=1, source_target_pairs={{16,0},{128,16},{144,128},{0,144},{17,1},{129,17},{145,129},{1,145... | collective-permute-start | bytes 983048 | tf_op jit(solution)/shard_map/ppermute | solution.py:270
  62.7 0.8 collective-permute-done.1.b_ref
  63.5 0.1 add.1.own_ref
  63.6 6.8 %collective-permute-done.5.b_ref = bf16[128,1280]{1,0:T(8,128)(2,1)S(1)} collective-permute-done((bf16[128,1280]{1,0:T(8,128)(2,1)S(1)}, bf16[128,1280]{1,0:T(8,128)(2,1)S(1)}, u32[]{:S(2)}, u32[]{:S(2)}) %collective-permute-start.5) | collective-permute-done | bytes 327712 | tf_op jit(solution)/shard_map/ppermute | solution.py:270
  70.4 0.1 collective-permute-done.3.a_ref
  70.5 0.2 join.1
  70.7 27.1 %all_to_all.11.slots_ref = bf16[64,2,2,1280]{3,2,1,0:T(2,128)(2,1)S(1)} all-to-all(bf16[64,2,2,1280]{3,2,1,0:T(2,128)(2,1)S(1)} %join.1), channel_id=1, replica_groups=mesh['dp'=2,'x'=4,'y_lo'=2,'z'=8,'core'=2] {'x','z','core'}, dimensions={0} | all-to-all | bytes 1310720 | tf_op jit(solution)/shard_map/all_to_all | solution.py:274
  97.7 0.0 copy-done.2
  97.7 1.4 %mix.1 = bf16[2,256,1280]{2,1,0:T(8,128)(2,1)} custom-call(bf16[2,256,256]{2,1,0:T(8,128)(2,1)S(1)} %copy-done.2, bf16[64,2,2,1280]{3,2,1,0:T(2,128)(2,1)S(1)} %all_to_all.11.slots_ref), custom_call_target="tpu_custom_call" | custom-call | tf_op jit(solution)/shard_map/mix/pallas_call | solution.py:257
Async XLA Ops:
  0.0 44.5 %copy-start = (bf16[1,1280,1280]{2,1,0:T(8,128)(2,1)S(1)}, bf16[1,1280,1280]{2,1,0:T(8,128)(2,1)}, u32[]{:S(2)}) copy-start(bf16[1,1280,1280]{2,1,0:T(8,128)(2,1)} %up_hbm.1) | copy-start | bytes 9830404
  38.8 10.6 %collective-permute-start = (bf16[128,1280]{1,0:T(8,128)(2,1)S(1)}, bf16[128,1280]{1,0:T(8,128)(2,1)S(1)}, u32[]{:S(2)}, u32[]{:S(2)}) collective-permute-start(bf16[128,1280]{1,0:T(8,128)(2,1)S(1)} %get-tuple-element.16.rows_ref), channel_id=1, source_target_pairs={{0,128},{16,144},{128,0},{144,16},{1,129},{17,145},{129,1},{145,17... | collective-permute-start | bytes 983048 | tf_op jit(solution)/shard_map/ppermute | solution.py:270
  41.8 15.8 %collective-permute-start.2 = (bf16[128,1280]{1,0:T(8,128)(2,1)S(1)}, bf16[128,1280]{1,0:T(8,128)(2,1)S(1)}, u32[]{:S(2)}, u32[]{:S(2)}) collective-permute-start(bf16[128,1280]{1,0:T(8,128)(2,1)S(1)} %get-tuple-element.20), channel_id=1, source_target_pairs={{0,16},{16,128},{128,144},{144,0},{1,17},{17,129},{129,145},{145,1... | collective-permute-start | bytes 983048 | tf_op jit(solution)/shard_map/ppermute | solution.py:270
  42.2 16.6 %collective-permute-start.4 = (bf16[128,1280]{1,0:T(8,128)(2,1)S(1)}, bf16[128,1280]{1,0:T(8,128)(2,1)S(1)}, u32[]{:S(2)}, u32[]{:S(2)}) collective-permute-start(bf16[128,1280]{1,0:T(8,128)(2,1)S(1)} %get-tuple-element.20), channel_id=1, source_target_pairs={{0,144},{16,0},{128,16},{144,128},{1,145},{17,1},{129,17},{145,129... | collective-permute-start | bytes 983048 | tf_op jit(solution)/shard_map/ppermute | solution.py:270
  44.5 1.9 %copy-start.1 = (bf16[1,1280,1280]{2,1,0:T(8,128)(2,1)S(1)}, bf16[1,1280,1280]{2,1,0:T(8,128)(2,1)}, u32[]{:S(2)}) copy-start(bf16[1,1280,1280]{2,1,0:T(8,128)(2,1)} %down_hbm.1) | copy-start | bytes 9830404
  50.6 12.9 %collective-permute-start.1 = (bf16[128,1280]{1,0:T(8,128)(2,1)S(1)}, bf16[128,1280]{1,0:T(8,128)(2,1)S(1)}, u32[]{:S(2)}, u32[]{:S(2)}) collective-permute-start(bf16[128,1280]{1,0:T(8,128)(2,1)S(1)} %expert.3), channel_id=1, source_target_pairs={{128,0},{144,16},{0,128},{16,144},{129,1},{145,17},{1,129},{17,145... | collective-permute-start | bytes 983048 | tf_op jit(solution)/shard_map/ppermute | solution.py:270
  60.0 37.7 %copy-start.2 = (bf16[2,256,256]{2,1,0:T(8,128)(2,1)S(1)}, bf16[2,256,256]{2,1,0:T(8,128)(2,1)}, u32[]{:S(2)}) copy-start(bf16[2,256,256]{2,1,0:T(8,128)(2,1)} %get-tuple-element.14.combine_ref) | copy-start | bytes 786436
  60.0 10.4 %collective-permute-start.5 = (bf16[128,1280]{1,0:T(8,128)(2,1)S(1)}, bf16[128,1280]{1,0:T(8,128)(2,1)S(1)}, u32[]{:S(2)}, u32[]{:S(2)}) collective-permute-start(bf16[128,1280]{1,0:T(8,128)(2,1)S(1)} %expert.5), channel_id=1, source_target_pairs={{144,0},{0,16},{16,128},{128,144},{145,1},{1,17},{17,129},{129,145... | collective-permute-start | bytes 983048 | tf_op jit(solution)/shard_map/ppermute | solution.py:270
  60.3 10.2 %collective-permute-start.3 = (bf16[128,1280]{1,0:T(8,128)(2,1)S(1)}, bf16[128,1280]{1,0:T(8,128)(2,1)S(1)}, u32[]{:S(2)}, u32[]{:S(2)}) collective-permute-start(bf16[128,1280]{1,0:T(8,128)(2,1)S(1)} %expert.4), channel_id=1, source_target_pairs={{16,0},{128,16},{144,128},{0,144},{17,1},{129,17},{145,129},{1,145... | collective-permute-start | bytes 983048 | tf_op jit(solution)/shard_map/ppermute | solution.py:270
